TPU v7x, 32 devices: a whole 2x2x4 slice. The times are simulated.
32 devices in a mesh: ser: 8 (over z, y), org: 4 (over x, core).
Axes of the slice: x: 2, y: 2, z: 4, core: 2. Of those that a mesh axis runs over, the one named last changes fastest.
Arguments:
- residual: float32 [64, 8192], P('org', 'ser'), may hold values from -48 to 48
- sub_size: int32 [16], replicated, may hold values from 256 to 1280, as said below
- sub_owner: int32 [16], replicated, may hold values from 0 to 7, as said below
- series_perm: int32 [8192], replicated, may hold values from 0 to 8191, as said below
Outputs:
- whitened: float32 [64, 8192], P('org', 'ser')
- log_diag: float32 [8, 2048], P('ser', 'org')
Inputs may be any that keep to these rules, and one draw needn't show every extreme that they name: `sub_size`: every size is a multiple of 256; the sizes sum to 8192. `sub_owner`: the subtrees of one owner hold at most 2048 series together; some owner holds exactly 2048. `series_perm`: A permutation of the series. Of the 1024 series of one index of ser, at most 256 lie in subtrees of any one owner; some owner receives exactly 256 from every index.
All inputs are finite; a program needn't handle non-finite values.
Results may differ from a plain program's by a relative error of at most 0.0003.
Values sent between devices are 32-bit elements; how exact they have to be, the bound alone decides.
No kernel may reach another device: no remote copies, remote signals or barrier semaphores. Data moves between devices by JAX's collectives and lax.ppermute only.
A program may use at most 192 MiB of HBM per device.

v0:
```python
import jax
import jax.numpy as jnp
from jax import lax
from jax.sharding import PartitionSpec as P

SLOTS = 2048


epsilon = 1e-06


def slot_tables(sub_size, sub_owner, series_perm, owner_count, slot_count):
    subtree_count = sub_size.shape[0]
    series_count = series_perm.shape[0]
    end_pos = jnp.cumsum(sub_size)
    start_pos = end_pos - sub_size
    order_ids = jnp.arange(subtree_count, dtype=jnp.int32)
    earlier = (sub_owner[None, :] == sub_owner[:, None]) & (order_ids[None, :] < order_ids[:, None])
    slot_start = jnp.sum(jnp.where(earlier, sub_size[None, :], 0), axis=1)
    position = jnp.arange(series_count, dtype=jnp.int32)
    subtree_of = jnp.sum((position[:, None] >= end_pos[None, :]).astype(jnp.int32), axis=1)
    placed = (
        sub_owner[subtree_of] * slot_count
        + slot_start[subtree_of]
        + position
        - start_pos[subtree_of]
    )
    empty_table = jnp.full((owner_count * slot_count,), -1, jnp.int32)
    slot_series = empty_table.at[placed].set(series_perm)
    slot_subtree = empty_table.at[placed].set(subtree_of)
    return (
        slot_series.reshape(owner_count, slot_count),
        slot_subtree.reshape(owner_count, slot_count),
    )


def gram_only(block):
    dims = (((0,), (0,)), ((), ()))
    return lax.dot_general(
        block, block, dims, precision=lax.Precision.HIGHEST, preferred_element_type=jnp.float32
    )


def tree_cross(block, inv_square, member):
    highest = lax.Precision.HIGHEST
    squared = block * block
    scaled = squared * inv_square[None, :]
    tree_total = jnp.dot(scaled, member, precision=highest)
    spread_back = lax.dot_general(
        tree_total,
        member,
        (((1,), (1,)), ((), ())),
        precision=highest,
        preferred_element_type=jnp.float32,
    )
    return jnp.sum(squared * spread_back, axis=0) - jnp.sum(squared * scaled, axis=0)


def membership(slot_subtree, subtree_count):
    return (slot_subtree[:, None] == jnp.arange(subtree_count, dtype=jnp.int32)[None, :]).astype(
        jnp.float32
    )


def shrink_factor(gram_sum, cross, anchors, slot_subtree, member):
    highest = lax.Precision.HIGHEST
    filled = slot_subtree >= 0
    spread = jnp.diagonal(gram_sum) / anchors
    inv_scale = jnp.where(filled, lax.rsqrt(spread + epsilon), 0.0)
    slot_total = slot_subtree.shape[0]
    slot_ids = jnp.arange(slot_total, dtype=jnp.int32)
    on_diag = slot_ids[:, None] == slot_ids[None, :]
    same_tree = (
        (slot_subtree[:, None] == slot_subtree[None, :])
        & filled[:, None]
        & jnp.logical_not(on_diag)
    )
    correl = gram_sum / anchors * inv_scale[:, None] * inv_scale[None, :]
    lower_sum = jnp.sum(jnp.where(same_tree, correl * correl, 0.0), axis=1)
    upper_sum = jnp.where(
        filled, (inv_scale * inv_scale / anchors * cross - lower_sum) / (anchors - 1), 0.0
    )
    upper_tree = jnp.dot(upper_sum, member, precision=highest)
    lower_tree = jnp.dot(lower_sum, member, precision=highest)
    upper_slot = jnp.dot(member, upper_tree, precision=highest)
    lower_slot = jnp.dot(member, lower_tree, precision=highest)
    shrink = jnp.minimum(upper_slot / jnp.where(filled, lower_slot, 1.0), 1.0)
    diag_value = jnp.where(filled, spread, 1.0)
    weight = jnp.where(
        on_diag,
        diag_value[:, None],
        jnp.where(same_tree, (1.0 - shrink)[:, None] * (gram_sum / anchors), 0.0),
    )
    return jnp.linalg.cholesky(weight)


def pick_columns(block, table):
    padded = jnp.concatenate([block, jnp.zeros((block.shape[0], 1), block.dtype)], axis=1)
    return jnp.take(padded, table, axis=1)


def per_device(residual, sub_size, sub_owner, series_perm):
    owner_count = lax.axis_size("ser")
    owner_here = lax.axis_index("ser")
    org_count = lax.axis_size("org")
    org_here = lax.axis_index("org")
    t_dev, ser_dev = residual.shape
    subtree_count = sub_size.shape[0]
    per_peer = SLOTS // owner_count
    dummy_send = owner_count * per_peer
    slot_series, slot_subtree = slot_tables(sub_size, sub_owner, series_perm, owner_count, SLOTS)
    filled_all = slot_series >= 0
    source_all = jnp.where(filled_all, slot_series // ser_dev, -1)
    from_here = source_all == owner_here
    send_rank = jnp.cumsum(from_here.astype(jnp.int32), axis=1) - 1
    send_slot = jnp.where(
        from_here,
        jnp.arange(owner_count, dtype=jnp.int32)[:, None] * per_peer + send_rank,
        dummy_send,
    )
    local_row = slot_series - owner_here * ser_dev
    send_table = (
        jnp.full((dummy_send + 1,), ser_dev, jnp.int32)
        .at[send_slot.reshape(-1)]
        .set(local_row.reshape(-1))[:dummy_send]
    )
    my_series = lax.dynamic_index_in_dim(slot_series, owner_here, 0, keepdims=False)
    my_subtree = lax.dynamic_index_in_dim(slot_subtree, owner_here, 0, keepdims=False)
    my_filled = my_series >= 0
    my_source = jnp.where(my_filled, my_series // ser_dev, 0)
    hits = (
        (my_source[:, None] == jnp.arange(owner_count, dtype=jnp.int32)[None, :])
        & my_filled[:, None]
    ).astype(jnp.int32)
    recv_rank = jnp.sum(jnp.cumsum(hits, axis=0) * hits, axis=1) - 1
    recv_index = jnp.where(my_filled, my_source * per_peer + recv_rank, dummy_send)
    member = membership(my_subtree, subtree_count)
    all_anchors = lax.all_gather(residual, "org", axis=0, tiled=True)
    anchors = all_anchors.shape[0]
    incoming = lax.all_to_all(
        pick_columns(all_anchors, send_table), "ser", split_axis=1, concat_axis=1, tiled=True
    )
    gathered = pick_columns(incoming, recv_index)
    gram_sum = gram_only(gathered)
    inv_scale = jnp.where(my_filled, lax.rsqrt(jnp.diagonal(gram_sum) / anchors + epsilon), 0.0)
    cross = tree_cross(gathered, inv_scale * inv_scale, member)
    arrived = lax.dynamic_slice_in_dim(gathered, org_here * t_dev, t_dev, 0)
    lower = shrink_factor(gram_sum, cross, anchors, my_subtree, member)
    whitened_slots = lax.linalg.triangular_solve(
        lower, arrived, left_side=False, lower=True, transpose_a=True
    )
    log_all = jnp.log(jnp.diagonal(lower))
    share = SLOTS // org_count
    log_part = lax.dynamic_slice_in_dim(log_all, org_here * share, share, 0)[None, :]
    back_table = (
        jnp.full((dummy_send + 1,), SLOTS, jnp.int32)
        .at[recv_index]
        .set(jnp.arange(SLOTS, dtype=jnp.int32))[:dummy_send]
    )
    returned = lax.all_to_all(
        pick_columns(whitened_slots, back_table), "ser", split_axis=1, concat_axis=1, tiled=True
    )
    row_place = (
        jnp.zeros((ser_dev + 1,), jnp.int32)
        .at[send_table]
        .set(jnp.arange(dummy_send, dtype=jnp.int32))[:ser_dev]
    )
    whitened = jnp.take(returned, row_place, axis=1)
    return (whitened, log_part)


def solution(mesh):
    in_specs = (P("org", "ser"), P(), P(), P())
    out_specs = (P("org", "ser"), P("ser", "org"))
    return jax.shard_map(
        per_device, mesh=mesh, in_specs=in_specs, out_specs=out_specs, check_vma=False
    )
```

profile of v0, /device:TPU:0, one launch (start us, length us, event | category | flops | bytes accessed | tf_op | source)
XLA Modules:
  0.0 1116.7 jit_solution(10650026727195678495)
XLA Ops:
  12.0 8.8 select_select_fusion.2
  20.8 5.8 select_select_fusion.4
  26.6 11.3 %select_add_fusion = s32[8192]{0:T(1024)S(1)} fusion(pred[8192]{0:T(1024)(128)(4,1)S(1)} %get-tuple-element.26, pred[8192]{0:T(1024)(128)(4,1)S(1)} %get-tuple-element.25, pred[8192]{0:T(1024)(128)(4,1)S(1)} %get-tuple-element.22, pred[8192]{0:T(1024)(128)(4,1)S(1)} %get-tuple-element.23, pred[8192]{0:T(1024)(128)(4,1)S(1)} %get-tuple-element.24, ...), kind=kLoop, calls=%fused_computation.428 | loop fusion | flops 163840 | bytes 172104 | tf_op jit(solution)/shard_map/add | solution.py:23
  38.0 30.7 %scatter_custom_fusion = s32[16384]{0:T(1024)S(1)} fusion(s32[8192]{0:T(1024)S(1)} %bitcast.360, s32[8192]{0:T(1024)} %param.7, s32[]{:T(128)} %constant.659.clone.1), kind=kCustom, calls=%fused_computation.434 | custom fusion | bytes 66048 | tf_op jit(solution)/shard_map/scatter | solution.py:29
  71.7 60.3 %scatter_custom_fusion.1 = s32[2049]{0:T(1024)S(1)} fusion(s32[16384]{0:T(1024)S(1)} %get-tuple-element.94, s32[16384]{0:T(1024)S(1)} %get-tuple-element.93, s32[]{:T(128)} %constant.658.clone.1), kind=kCustom, calls=%fused_computation.500 | custom fusion | bytes 8200 | tf_op jit(solution)/shard_map/scatter | solution.py:125
  132.1 7.4 all_gather.3
  139.8 5.5 gather_fusion
  146.4 5.9 all-to-all-start
  155.4 8.1 scatter_custom_fusion.3
  163.5 30.5 %scatter_custom_fusion.4 = s32[16384]{0:T(1024)S(1)} fusion(s32[8192]{0:T(1024)S(1)} %bitcast.361, s32[8192]{0:T(1024)S(1)} %convert_reduce_fusion, s32[]{:T(128)} %constant.659.clone.1), kind=kCustom, calls=%fused_computation.432 | custom fusion | bytes 65540 | tf_op jit(solution)/shard_map/scatter | solution.py:30
  194.1 8.5 scatter_custom_fusion.2
  203.1 5.5 gather_fusion.1
  208.9 16.0 %fusion.217 = f32[2048,2048]{0,1:T(8,128)} fusion(f32[2048,64]{0,1:T(8,128)S(1)} %broadcast_select_fusion), kind=kOutput, calls=%fused_computation.557 | convolution fusion | flops 3221225472 | bytes 17301504 | tf_op jit(solution)/shard_map/dot_general | solution.py:39
  224.9 17.6 %copy.38 = f32[2048,2048]{1,0:T(8,128)} copy(f32[2048,2048]{0,1:T(8,128)} %fusion.217) | data formatting | bytes 33554432 | tf_op jit(solution)/shard_map/dot_general | solution.py:39
  242.5 34.1 %gather_fusion.2 = f32[2048]{0:T(1024)S(1)} fusion(f32[2048,2048]{0,1:T(8,128)} %fusion.217, s32[2048]{0:T(1024)S(1)} %bitcast.328), kind=kCustom, calls=%fused_computation.2 | custom fusion | bytes 32768 | tf_op jit(solution)/shard_map/jit(diagonal)/cond/branch_0_fun/gather | solution.py:68
  278.1 12.3 %select_reduce_fusion = f32[2048]{0:T(1024)S(1)} fusion(f32[2048,2048]{1,0:T(8,128)} %copy.38, f32[2048]{0:T(1024)S(1)} %bitcast.356, f32[2048]{0:T(1024)S(1)} %select_multiply_fusion.1, s32[2048]{0:T(1024)S(1)} %bitcast.337, pred[2048]{0:T(1024)(128)(4,1)S(1)} %get-tuple-element.38), kind=kLoop, calls=%fused_computation.17 | loop fusion | flops 41940992 | bytes 16812032 | tf_op jit(solution)/shard_map/reduce_sum | solution.py:79
  294.0 6.2 multiply_bitcast_fusion
  300.2 17.6 %copy.39 = f32[2048,2048]{1,0:T(8,128)} copy(f32[2048,2048]{0,1:T(8,128)} %multiply_bitcast_fusion) | data formatting | bytes 33554432 | tf_op jit(solution)/shard_map/mul | solution.py:92
  317.8 22.9 %add_multiply_fusion = f32[2048,2048]{1,0:T(8,128)S(1)} fusion(f32[2048,2048]{1,0:T(8,128)} %copy.39, f32[2048,2048]{1,0:T(8,128)} %copy.38, f32[2048]{0:T(1024)S(1)} %get-tuple-element.37, f32[2048]{0:T(1024)S(1)} %subtract_multiply_fusion, s32[2048]{0:T(1024)S(1)} %bitcast.343, pred[2048]{0:T(1024)(128)(4,1)S(1)} %get-tuple-element.38), kind=kLoop, calls=%fused_computation.14 | loop fusion | flops 71303168 | bytes 50358272 | tf_op jit(solution)/shard_map/jit(cholesky)/div | solution.py:94
  340.7 5.7 copy-done.1
  346.5 11.7 %cholesky.456 = f32[128,128]{1,0:T(8,128)S(1)} custom-call(f32[128,128]{1,0:T(8,128)S(1)} %cholesky.1201), custom_call_target="Cholesky" | custom-call | tf_op jit(solution)/shard_map/jit(cholesky)/cholesky | solution.py:94
  358.2 7.8 cholesky.486
  366.0 9.8 custom-call.126
  381.2 11.9 %cholesky.479 = f32[128,128]{1,0:T(8,128)S(1)} custom-call(f32[128,128]{1,0:T(8,128)S(1)} %cholesky.1205), custom_call_target="Cholesky" | custom-call | tf_op jit(solution)/shard_map/jit(cholesky)/cholesky | solution.py:94
  395.0 9.8 custom-call.127
  410.1 11.7 %cholesky.502 = f32[128,128]{1,0:T(8,128)S(1)} custom-call(f32[128,128]{1,0:T(8,128)S(1)} %cholesky.1210), custom_call_target="Cholesky" | custom-call | tf_op jit(solution)/shard_map/jit(cholesky)/cholesky | solution.py:94
  423.2 9.8 custom-call.128
  439.7 11.7 %cholesky.523 = f32[128,128]{1,0:T(8,128)S(1)} custom-call(f32[128,128]{1,0:T(8,128)S(1)} %cholesky.1215), custom_call_target="Cholesky" | custom-call | tf_op jit(solution)/shard_map/jit(cholesky)/cholesky | solution.py:94
  452.8 9.8 custom-call.129
  469.3 11.7 %cholesky.960 = f32[128,128]{1,0:T(8,128)S(1)} custom-call(f32[128,128]{1,0:T(8,128)S(1)} %cholesky.1220), custom_call_target="Cholesky" | custom-call | tf_op jit(solution)/shard_map/jit(cholesky)/cholesky | solution.py:94
  482.4 9.8 custom-call.130
  493.8 5.5 fusion.33
  499.4 11.9 %cholesky.980 = f32[128,128]{1,0:T(8,128)S(1)} custom-call(f32[128,128]{1,0:T(8,128)S(1)} %cholesky.1225), custom_call_target="Cholesky" | custom-call | tf_op jit(solution)/shard_map/jit(cholesky)/cholesky | solution.py:94
  512.6 9.8 custom-call.131
  524.0 5.7 fusion.30
  529.6 11.7 %cholesky.1000 = f32[128,128]{1,0:T(8,128)S(1)} custom-call(f32[128,128]{1,0:T(8,128)S(1)} %cholesky.1230), custom_call_target="Cholesky" | custom-call | tf_op jit(solution)/shard_map/jit(cholesky)/cholesky | solution.py:94
  542.7 10.2 custom-call.132
  554.4 6.2 fusion.27
  560.6 11.7 %cholesky.1020 = f32[128,128]{1,0:T(8,128)S(1)} custom-call(f32[128,128]{1,0:T(8,128)S(1)} %cholesky.1235), custom_call_target="Cholesky" | custom-call | tf_op jit(solution)/shard_map/jit(cholesky)/cholesky | solution.py:94
  573.6 10.0 custom-call.133
  585.0 5.9 fusion.45
  590.9 11.7 %cholesky.1040 = f32[128,128]{1,0:T(8,128)S(1)} custom-call(f32[128,128]{1,0:T(8,128)S(1)} %cholesky.1240), custom_call_target="Cholesky" | custom-call | tf_op jit(solution)/shard_map/jit(cholesky)/cholesky | solution.py:94
  603.9 9.8 custom-call.134
  615.1 6.3 fusion.48
  621.3 11.7 %cholesky.1060 = f32[128,128]{1,0:T(8,128)S(1)} custom-call(f32[128,128]{1,0:T(8,128)S(1)} %cholesky.1245), custom_call_target="Cholesky" | custom-call | tf_op jit(solution)/shard_map/jit(cholesky)/cholesky | solution.py:94
  634.4 9.8 custom-call.135
  645.4 6.0 fusion.51
  651.5 11.7 %cholesky.1080 = f32[128,128]{1,0:T(8,128)S(1)} custom-call(f32[128,128]{1,0:T(8,128)S(1)} %cholesky.1250), custom_call_target="Cholesky" | custom-call | tf_op jit(solution)/shard_map/jit(cholesky)/cholesky | solution.py:94
  664.5 9.8 custom-call.136
  680.8 11.9 %cholesky.1100 = f32[128,128]{1,0:T(8,128)S(1)} custom-call(f32[128,128]{1,0:T(8,128)S(1)} %cholesky.1255), custom_call_target="Cholesky" | custom-call | tf_op jit(solution)/shard_map/jit(cholesky)/cholesky | solution.py:94
  694.0 9.8 custom-call.137
  709.6 11.7 %cholesky.1120 = f32[128,128]{1,0:T(8,128)S(1)} custom-call(f32[128,128]{1,0:T(8,128)S(1)} %cholesky.1260), custom_call_target="Cholesky" | custom-call | tf_op jit(solution)/shard_map/jit(cholesky)/cholesky | solution.py:94
  722.6 10.0 custom-call.138
  737.9 11.7 %cholesky.1140 = f32[128,128]{1,0:T(8,128)S(1)} custom-call(f32[128,128]{1,0:T(8,128)S(1)} %cholesky.1265), custom_call_target="Cholesky" | custom-call | tf_op jit(solution)/shard_map/jit(cholesky)/cholesky | solution.py:94
  750.9 9.8 custom-call.139
  765.1 12.1 %cholesky.1160 = f32[128,128]{1,0:T(8,128)S(1)} custom-call(f32[128,128]{1,0:T(8,128)S(1)} %cholesky.1270), custom_call_target="Cholesky" | custom-call | tf_op jit(solution)/shard_map/jit(cholesky)/cholesky | solution.py:94
  778.5 9.8 custom-call.140
  791.8 11.7 %cholesky.1178 = f32[128,128]{1,0:T(8,128)S(1)} custom-call(f32[128,128]{1,0:T(8,128)S(1)} %convolution_subtract_fusion.2), custom_call_target="Cholesky" | custom-call | tf_op jit(solution)/shard_map/jit(cholesky)/cholesky | solution.py:94
  814.8 18.0 %fusion.2 = (f32[2048,2048]{1,0:T(8,128)}, f32[2048,2048]{1,0:T(8,128)}) fusion(f32[2048,2048]{1,0:T(8,128)} %get-tuple-element.48, pred[]{:T(512)S(6)} %cholesky.1200), kind=kLoop, calls=%fused_computation.21 | loop fusion | flops 16777216 | bytes 50331648 | tf_op jit(solution)/shard_map/triangular_solve | solution.py:149
  832.8 47.8 %while.1 = (s32[]{:T(128)}, f32[2048,2048]{1,0:T(8,128)}, s32[16,2]{0,1:T(2,128)S(1)}, f32[16,128,128]{2,1,0:T(8,128)S(1)}, s32[]{:T(128)}) while((s32[]{:T(128)}, f32[2048,2048]{1,0:T(8,128)}, s32[16,2]{0,1:T(2,128)S(1)}, f32[16,128,128]{2,1,0:T(8,128)S(1)}, s32[]{:T(128)}) %tuple.237), condition=%wide.while_cond, body=%wide.while_body.sunk | while | flops 2 | bytes 131181 | solution.py:149
  880.6 157.3 %custom-call.141 = f32[16,128,128]{1,2,0:T(8,128)S(1)} custom-call(f32[16,128,128]{2,1,0:T(8,128)S(1)} %get-tuple-element.9), custom_call_target="InvertDiagBlocksLowerTriangular" | custom-call | tf_op jit(solution)/shard_map/triangular_solve | solution.py:149
  1065.1 5.5 gather_fusion.3
  1071.6 6.0 all-to-all-start.1
  1077.6 34.1 %gather_fusion.5 = f32[2048]{0:T(1024)S(1)} fusion(f32[2048,2048]{1,0:T(8,128)} %get-tuple-element.36, s32[2048]{0:T(1024)S(1)} %bitcast.329), kind=kCustom, calls=%fused_computation.5 | custom fusion | bytes 32768 | tf_op jit(solution)/shard_map/jit(diagonal)/cond/branch_0_fun/gather | solution.py:152
  (236 shorter events, 183.7 us)
Async XLA Ops:
  146.4 56.2 %all-to-all-start = ((f32[64,8,256]{2,0,1:T(8,128)}), f32[64,8,256]{2,0,1:T(8,128)S(1)}, u32[]{:S(2)}, u32[]{:S(2)}) async-start(f32[64,8,256]{2,0,1:T(8,128)} %broadcast_select_fusion.1), calls=%async_computation | async-start | bytes 1048576 | tf_op jit(solution)/shard_map/all_to_all | solution.py:140
  276.6 17.4 %copy-start = (f32[2048,2048]{1,0:T(8,128)S(1)}, f32[2048,2048]{1,0:T(8,128)}, u32[]{:S(2)}) copy-start(f32[2048,2048]{1,0:T(8,128)} %copy.38) | copy-start | bytes 50331652
  340.7 5.7 copy-start.1
  1071.6 40.8 %all-to-all-start.1 = ((f32[16,8,256]{2,0,1:T(8,128)}), f32[16,8,256]{2,0,1:T(8,128)S(1)}, u32[]{:S(2)}, u32[]{:S(2)}) async-start(f32[16,8,256]{2,0,1:T(8,128)} %broadcast_select_fusion.2), calls=%async_computation.1 | async-start | bytes 262144 | tf_op jit(solution)/shard_map/all_to_all | solution.py:160
where the time goes:
time: 1130 us; the launch traced here: 1120 us
  other arithmetic  614 us (54%)
  local copies, waits for them, and re-layouts  330 us (29%)
  matrix products  141 us (12%)
  starting transfers between devices  11.9 us (1%)
  between operations  11.8 us (1%)
    another operation x63, other arithmetic, shrink_factor(): return jnp.linalg.cholesky(weight)  357 us
    another operation x3, other arithmetic, per_device(): lax.linalg.triangular_solve(lower, arrived, left_side=False, lower=True,...  175 us
    another operation x30, matrix products, shrink_factor(): return jnp.linalg.cholesky(weight)  93.6 us
    scatter x1, local copies, waits for them, and re-layouts, per_device(): send_table = jnp.full((dummy_send + 1,), ser_dev, jnp.int32).at[send_slot...  60.3 us
    another operation x51, local copies, waits for them, and re-layouts  48.8 us
    gather x1, local copies, waits for them, and re-layouts, per_device(): log_all = jnp.log(jnp.diagonal(lower))  34.1 us
    gather x1, local copies, waits for them, and re-layouts, shrink_factor(): spread = jnp.diagonal(gram_sum) / anchors  34.1 us
    scatter x1, local copies, waits for them, and re-layouts, slot_tables(): slot_series = empty_table.at[placed].set(series_perm)  30.7 us
  transfers between devices with their start and end apart: 2, of which 0 were waited for; matrix products, arithmetic and copies ran while one was open for 8% of the time, Pallas kernels for 0%

commit v1 on v0

v1 whole, which is shorter than its diff:
```python
import functools

import jax
import jax.numpy as jnp
from jax import lax
from jax.experimental import pallas as pl
from jax.experimental.pallas import tpu as pltpu
from jax.sharding import PartitionSpec as P

SLOTS = 2048
TILE = 256
LANES = 128
ROWS = TILE // LANES
BLOCK = 64
OWNER_TILES = SLOTS // TILE

epsilon = 1e-06

NN = (((1,), (0,)), ((), ()))
NT = (((1,), (1,)), ((), ()))


def dot_bf16(left, right, dims=NN):
    return lax.dot_general(left, right, dims, preferred_element_type=jnp.float32)


def dot_f32(left, right, dims=NN):
    return lax.dot_general(
        left, right, dims, precision=lax.Precision.HIGHEST, preferred_element_type=jnp.float32
    )


def as_bf16(mask):
    return jnp.where(mask, 1.0, 0.0).astype(jnp.bfloat16)


def split_three(value):
    high = value.astype(jnp.bfloat16)
    rest = value - high.astype(jnp.float32)
    middle = rest.astype(jnp.bfloat16)
    low = (rest - middle.astype(jnp.float32)).astype(jnp.bfloat16)
    return jnp.concatenate([high, middle, low], axis=0)


def join_three(value):
    rows = value.shape[0] // 3
    return value[:rows] + value[rows : 2 * rows] + value[2 * rows :]


def iota(shape, dim):
    return lax.broadcasted_iota(jnp.int32, shape, dim)


def before_in_row(width):
    return as_bf16(iota((LANES, width), 0) < iota((LANES, width), 1))


def pack_body(
    size_ref, owner_ref, x_ref, perm_ref, send_ref, dest_ref, place_ref, *, n_ser, n_org
):
    here = lax.axis_index("ser")
    n_sub = size_ref.shape[0]
    rows = perm_ref.shape[0]
    t_dev, ser_dev = x_ref.shape
    per_peer = SLOTS // n_ser
    shift = ser_dev.bit_length() - 1
    groups = ser_dev // LANES

    def owner_of(row_ids):
        owner = jnp.zeros(row_ids.shape, jnp.int32)
        start = jnp.int32(0)
        for k in range(n_sub):
            owner = jnp.where(row_ids >= start, owner_ref[k], owner)
            start = start + (size_ref[k] >> 7)
        return owner

    owner_down = owner_of(iota((rows, LANES), 0))
    owner_across = owner_of(iota((1, rows), 1))
    down_wide = owner_down[:, :rows] if rows <= LANES else owner_of(iota((rows, rows), 0))
    earlier = as_bf16(
        (down_wide == owner_across) & (iota((rows, rows), 1) < iota((rows, rows), 0))
    )
    mine = as_bf16((perm_ref[...] >> shift) == here)
    in_row = dot_bf16(mine, before_in_row(LANES))
    ahead = dot_bf16(earlier, mine).astype(jnp.bfloat16)
    in_rows = dot_bf16(ahead, jnp.ones((LANES, LANES), jnp.bfloat16))
    place_ref[...] = owner_down * per_peer + (in_row + in_rows).astype(jnp.int32)

    def to_local(g, total):
        at = pl.ds(pl.multiple_of(g * 8, 8), 8)
        series = perm_ref[at, :]
        place = place_ref[at, :]
        local = series & (ser_dev - 1)
        group = jnp.where((series >> shift) == here, local >> 7, -1)
        lane = local & (LANES - 1)
        upper = (place >> 4).astype(jnp.float32)
        lower = (place & 15).astype(jnp.float32)
        lefts, rights = [], []
        for s in range(8):
            hit = iota((groups, LANES), 0) == group[s : s + 1]
            lefts.append(
                jnp.concatenate(
                    [jnp.where(hit, upper[s : s + 1], 0.0), jnp.where(hit, lower[s : s + 1], 0.0)],
                    axis=0,
                ).astype(jnp.bfloat16)
            )
            rights.append(as_bf16(iota((LANES, LANES), 0) == lane[s : s + 1]))
        return total + dot_bf16(
            jnp.concatenate(lefts, axis=1), jnp.concatenate(rights, axis=1), NT
        )

    found = lax.fori_loop(0, rows // 8, to_local, jnp.zeros((2 * groups, LANES), jnp.float32))
    dest = (found[:groups] * 16.0 + found[groups:]).astype(jnp.int32)
    dest_ref[...] = dest
    terms = split_three(x_ref[...])

    def pack(o, carry):
        target = iota((per_peer, LANES), 0) + o * per_peer
        pick = jnp.concatenate([as_bf16(target == dest[h : h + 1]) for h in range(groups)], axis=1)
        columns = join_three(dot_bf16(terms, pick, NT))
        for r in range(n_org):
            send_ref[o * n_org + r] = columns
        return carry

    lax.fori_loop(0, n_ser, pack, 0)


def lane_pick(value, index):
    return jnp.take_along_axis(value, index, axis=1, mode="promise_in_bounds")


def eliminate(parts, size, whole):
    lane = iota((8, LANES), 1)
    sub = iota((8, LANES), 0)
    shift = lane & (LANES - size)
    parts = [list(part) for part in parts]
    downs = [[jnp.ones((8, LANES), jnp.float32)] * len(part) for part in parts]
    acrosses = [jnp.ones((8, LANES), jnp.float32) for _ in parts]
    for j in range(0, size, 2):
        g, s = divmod(j, 8)
        column0 = shift + j
        column1 = shift + (j + 1)
        on0, on1 = lane == column0, lane == column1
        on = on0 | on1
        for p, part in enumerate(parts):
            row0 = jnp.broadcast_to(part[g][s : s + 1], (8, LANES))
            row1 = jnp.broadcast_to(part[g][s + 1 : s + 2], (8, LANES))
            first = lane_pick(row0, column0)
            cross = lane_pick(row0, column1)
            second = lane_pick(row1, column1)
            row0 = jnp.where(on, jnp.where(on0, 1.0, 0.0), row0)
            row1 = jnp.where(on, jnp.where(on1, 1.0, 0.0), row1)
            inv = 1.0 / first
            step = cross * inv
            pivot = second - step * cross
            inv1 = 1.0 / pivot
            next1 = row1 - step * row0
            solved1 = next1 * inv1
            solved0 = row0 * inv - step * solved1
            for i in range(0 if whole else g, len(part)):
                old = part[i]
                new = (
                    jnp.where(on, 0.0, old)
                    - lane_pick(old, column0) * solved0
                    - lane_pick(old, column1) * solved1
                )
                if i == g:
                    if whole:
                        new = jnp.where(sub == s, solved0, jnp.where(sub == s + 1, solved1, new))
                    else:
                        new = jnp.where(sub <= s, old, jnp.where(sub == s + 1, next1, new))
                        new = jnp.where(sub == s, row0, new)
                part[i] = new
            if not whole:
                downs[p][g] = jnp.where(
                    sub == s, first, jnp.where(sub == s + 1, pivot, downs[p][g])
                )
                acrosses[p] = jnp.where(on0, first, jnp.where(on1, pivot, acrosses[p]))
    return parts, downs, acrosses


def owner_body(
    size_ref,
    owner_ref,
    recv_ref,
    perm_ref,
    back_ref,
    log_ref,
    all_ref,
    index_ref,
    pick_ref,
    inverse_ref,
    tile_ref,
    *,
    n_ser,
    n_org,
    ser_dev,
):
    here = lax.axis_index("ser")
    part = lax.axis_index("org")
    n_sub = size_ref.shape[0]
    t_dev = recv_ref.shape[1]
    anchors = t_dev * n_org
    per_peer = SLOTS // n_ser
    share = SLOTS // n_org
    tiles = share // TILE
    shift = ser_dev.bit_length() - 1
    slot_rows = SLOTS // LANES
    wide = max(per_peer, LANES)

    for t in range(OWNER_TILES):
        tile_ref[0, t] = jnp.int32(-1)
        tile_ref[1, t] = jnp.int32(0)
        tile_ref[2, t] = jnp.int32(0)
    at = jnp.int32(0)
    first = jnp.int32(0)
    for k in range(n_sub):
        count = size_ref[k] >> 8
        held = jnp.where(owner_ref[k] == here, count, 0)

        def put(i, carry, at=at, first=first, held=held):
            tile_ref[0, at + i] = first + i
            tile_ref[1, at + i] = at
            tile_ref[2, at + i] = at + held
            return carry

        lax.fori_loop(0, held, put, 0)
        at = at + held
        first = first + count

    for d in range(n_ser):
        for r in range(n_org):
            all_ref[r * t_dev : (r + 1) * t_dev, d * per_peer : (d + 1) * per_peer] = recv_ref[
                d * n_org + r
            ]

    pieces = []
    for t in range(OWNER_TILES):
        place = tile_ref[0, t]
        rows = perm_ref[pl.ds(jnp.maximum(place, 0) * ROWS, ROWS), :]
        pieces.append(jnp.where(place >= 0, rows, -1))
    source = jnp.concatenate(pieces, axis=0) >> shift
    from_peer = jnp.concatenate([as_bf16(source == d) for d in range(n_ser)], axis=0)
    in_row = dot_bf16(from_peer, before_in_row(LANES))
    row_total = dot_bf16(from_peer, jnp.ones((LANES, wide), jnp.bfloat16)).astype(jnp.bfloat16)
    span = n_ser * slot_rows
    left, right = iota((span, span), 0), iota((span, span), 1)
    ahead = as_bf16((left // slot_rows == right // slot_rows) & (right < left))
    base = dot_bf16(ahead, row_total)[:, :LANES]
    rank = jnp.zeros((slot_rows, LANES), jnp.float32)
    for d in range(n_ser):
        rows = slice(d * slot_rows, (d + 1) * slot_rows)
        rank = jnp.where(source == d, in_row[rows] + base[rows], rank)
    index_ref[...] = jnp.where(source >= 0, source * per_peer + rank.astype(jnp.int32), -1)
    left, right = iota((OWNER_TILES * n_ser, span), 0), iota((OWNER_TILES * n_ser, span), 1)
    through = as_bf16(
        (left % n_ser == right // slot_rows)
        & (right % slot_rows < ROWS * (left // n_ser) + ROWS)
    )
    ends = dot_bf16(through, row_total).astype(jnp.int32)[:, :per_peer]
    tile_of = jnp.zeros((n_ser, per_peer), jnp.int32)
    for t in range(OWNER_TILES):
        tile_of += (iota((n_ser, per_peer), 1) >= ends[t * n_ser : (t + 1) * n_ser]).astype(
            jnp.int32
        )
    tile_of = jnp.concatenate([tile_of[d : d + 1] for d in range(n_ser)], axis=1)

    block = all_ref[...]
    spread = jnp.sum(block * block, axis=0, keepdims=True) * (1.0 / anchors)
    scaled = block * jnp.where(spread > 0, lax.rsqrt(spread), 0.0)
    own = spread / (spread + epsilon)
    fourth = jnp.sum(jnp.square(scaled * scaled), axis=0, keepdims=True) * (1.0 / anchors)
    in_tree, ahead_of, filled = [], [], []
    for u in range(tiles):
        t = part * tiles + u
        low, high = tile_ref[1, t], tile_ref[2, t]
        filled.append(tile_ref[0, t] >= 0)
        in_tree.append((tile_of >= low) & (tile_of < high))
        ahead_of.append((tile_of >= low) & (tile_of < t))
    grams = dot_f32(
        jnp.concatenate(
            [scaled * jnp.where(mask, own, 0.0) for mask in in_tree]
            + [jnp.where(mask, scaled, 0.0) for mask in ahead_of],
            axis=0,
        ),
        scaled,
        NT,
    )
    unit = iota((anchors, anchors), 0) == iota((anchors, anchors), 1)
    shrink = []
    for u in range(tiles):
        dual = grams[u * anchors : (u + 1) * anchors] * (1.0 / anchors)
        own_square = jnp.where(in_tree[u], own * own, 0.0)
        square = dual * dual
        total = lambda value: jnp.sum(
            jnp.sum(value, axis=0, keepdims=True), axis=1, keepdims=True
        )
        lower = total(square) - total(own_square)
        upper = total(jnp.where(unit, square, 0.0)) * anchors - total(own_square * fourth)
        upper = (upper - lower) / (anchors - 1)
        shrink.append(jnp.where(filled[u], jnp.minimum(upper / jnp.where(filled[u], lower, 1.0), 1.0), 1.0))

    for i in range(share // LANES):
        row = index_ref[pl.ds(part * (tiles * ROWS) + i, 1), :]
        pick_ref[:, i * LANES : (i + 1) * LANES] = as_bf16(iota((SLOTS, LANES), 0) == row)
    mine = join_three(dot_bf16(split_three(block), pick_ref[...]))
    my_spread = jnp.sum(mine * mine, axis=0, keepdims=True) * (1.0 / anchors)
    mine = mine * jnp.where(my_spread > 0, lax.rsqrt(my_spread), 0.0)
    mine_down = mine.T

    per_tile = TILE // BLOCK
    blocks = share // BLOCK
    side = LANES // anchors
    rows_of = lambda b: slice(b * BLOCK, (b + 1) * BLOCK)
    for u in range(tiles):
        prior = grams[(tiles + u) * anchors : (tiles + u + 1) * anchors]
        gain = (1.0 - shrink[u]) * (1.0 / anchors)
        for v in range(per_tile):
            b = u * per_tile + v
            inverse_ref[b // side, :, (b % side) * anchors : (b % side + 1) * anchors] = (
                jnp.where(unit, shrink[u], 0.0) + gain * prior
            )
            if v < per_tile - 1:
                piece = mine[:, rows_of(b)]
                prior = prior + dot_f32(piece, piece, NT)

    inverses, _, _ = eliminate(
        [
            [inverse_ref[p, i * 8 : (i + 1) * 8, :] for i in range(anchors // 8)]
            for p in range(blocks // side)
        ],
        anchors,
        whole=True,
    )
    inverses = [jnp.concatenate(rows, axis=0) for rows in inverses]

    diagonal = iota((BLOCK, BLOCK), 0) == iota((BLOCK, BLOCK), 1)
    solved, weights = [], []
    for b in range(blocks):
        gain = (1.0 - shrink[b // per_tile]) * (1.0 / anchors)
        inverse = inverses[b // side][:, (b % side) * anchors : (b % side + 1) * anchors]
        solved.append(dot_f32(inverse, mine[:, rows_of(b)]))
        weights.append(
            jnp.where(diagonal, 1.0, 0.0) + gain * dot_f32(mine_down[rows_of(b)], solved[b])
        )
    pairs = [jnp.concatenate(weights[b : b + 2], axis=1) for b in range(0, blocks, 2)]
    lowers, downs, acrosses = eliminate(
        [[pair[i * 8 : (i + 1) * 8] for i in range(BLOCK // 8)] for pair in pairs],
        BLOCK,
        whole=False,
    )
    keep = iota((BLOCK, LANES), 0) >= (iota((BLOCK, LANES), 1) & (BLOCK - 1))
    done, logs = [], []
    for p in range(blocks // 2):
        lower = jnp.concatenate(
            [row * lax.rsqrt(pivot) for row, pivot in zip(lowers[p], downs[p])], axis=0
        )
        lower = jnp.where(keep, lower, 0.0)
        for h in range(2):
            b = 2 * p + h
            u = b // per_tile
            half = slice(h * BLOCK, (h + 1) * BLOCK)
            done.append(dot_f32(solved[b], lower[:, half], NT) * jnp.sqrt(shrink[u]))
            level = acrosses[p][:1, half] * my_spread[:, rows_of(b)] * shrink[u]
            logs.append(jnp.where(filled[u], 0.5 * jnp.log(level), 0.0))
    log_ref[...] = jnp.concatenate(logs, axis=1)
    terms = split_three(jnp.concatenate(done, axis=1))

    for d in range(n_ser):
        columns = join_three(
            dot_bf16(terms, pick_ref[d * per_peer : (d + 1) * per_peer, :], NT)
        )
        for r in range(n_org):
            back_ref[d * n_org + r] = columns[r * t_dev : (r + 1) * t_dev]


def home_body(back_ref, dest_ref, out_ref, *, n_ser, n_org):
    per_peer = back_ref.shape[2]
    pieces = []
    for o in range(n_ser):
        piece = back_ref[o * n_org]
        for q in range(1, n_org):
            piece = piece + back_ref[o * n_org + q]
        pieces.append(piece)
    terms = split_three(jnp.concatenate(pieces, axis=1))
    groups = dest_ref.shape[0]
    step = 2
    for h in range(0, groups, step):
        pick = jnp.concatenate(
            [
                as_bf16(iota((SLOTS, LANES), 0) == dest_ref[h + i : h + i + 1, :])
                for i in range(step)
            ],
            axis=1,
        )
        out_ref[:, h * LANES : (h + step) * LANES] = join_three(dot_bf16(terms, pick))


def per_device(residual, sub_size, sub_owner, series_perm):
    n_ser = lax.axis_size("ser")
    n_org = lax.axis_size("org")
    t_dev, ser_dev = residual.shape
    anchors = t_dev * n_org
    per_peer = SLOTS // n_ser
    share = SLOTS // n_org
    blocks = share // BLOCK
    side = LANES // anchors
    perm = series_perm.reshape(-1, LANES)
    vmem = pl.BlockSpec(memory_space=pltpu.VMEM)
    smem = pl.BlockSpec(memory_space=pltpu.SMEM)
    params = pltpu.CompilerParams(vmem_limit_bytes=48 * 1024 * 1024)
    blocks_shape = jax.ShapeDtypeStruct((n_ser * n_org, t_dev, per_peer), jnp.float32)

    send, dest = pl.pallas_call(
        functools.partial(pack_body, n_ser=n_ser, n_org=n_org),
        out_shape=(blocks_shape, jax.ShapeDtypeStruct((ser_dev // LANES, LANES), jnp.int32)),
        in_specs=[smem, smem, vmem, vmem],
        out_specs=(vmem, vmem),
        scratch_shapes=[pltpu.VMEM(perm.shape, jnp.int32)],
        compiler_params=params,
        name="pack",
    )(sub_size, sub_owner, residual, perm)
    recv = lax.all_to_all(send, ("ser", "org"), split_axis=0, concat_axis=0, tiled=True)
    back, log_part = pl.pallas_call(
        functools.partial(owner_body, n_ser=n_ser, n_org=n_org, ser_dev=ser_dev),
        out_shape=(blocks_shape, jax.ShapeDtypeStruct((1, share), jnp.float32)),
        in_specs=[smem, smem, vmem, vmem],
        out_specs=(vmem, vmem),
        scratch_shapes=[
            pltpu.VMEM((anchors, SLOTS), jnp.float32),
            pltpu.VMEM((SLOTS // LANES, LANES), jnp.int32),
            pltpu.VMEM((SLOTS, share), jnp.bfloat16),
            pltpu.VMEM((blocks // side, anchors, LANES), jnp.float32),
            pltpu.SMEM((3, OWNER_TILES), jnp.int32),
        ],
        compiler_params=params,
        name="owner",
    )(sub_size, sub_owner, recv, perm)
    returned = lax.all_to_all(back, ("ser", "org"), split_axis=0, concat_axis=0, tiled=True)
    whitened = pl.pallas_call(
        functools.partial(home_body, n_ser=n_ser, n_org=n_org),
        out_shape=jax.ShapeDtypeStruct((t_dev, ser_dev), jnp.float32),
        in_specs=[vmem, vmem],
        out_specs=vmem,
        compiler_params=params,
        name="home",
    )(returned, dest)
    return (whitened, log_part)


def solution(mesh):
    in_specs = (P("org", "ser"), P(), P(), P())
    out_specs = (P("org", "ser"), P("ser", "org"))
    return jax.shard_map(
        per_device, mesh=mesh, in_specs=in_specs, out_specs=out_specs, check_vma=False
    )
```

time: 1130 us -> 69.7 us (0.06); the launches traced: 1120 us -> 69.3 us
  other arithmetic: 614 us -> 0 us
  local copies, waits for them, and re-layouts: 330 us -> 2.28 us
  matrix products: 141 us -> 0 us
  blocking collectives: 7.41 us -> 41.1 us
  Pallas kernels: 0 us -> 25.3 us
  starting transfers between devices: 11.9 us -> 0 us
    another operation x72 -> x0, other arithmetic: 537 us -> none  [the longest x63 357 us: shrink_factor(): return jnp.linalg.cholesky(weight)]
    scatter x5 -> x0, local copies, waits for them, and re-layouts: 138 us -> none  [the longest x1 60.3 us: per_device(): send_table = jnp.full((dummy_send + 1,), ser_dev, jnp.int32).at[send_slot...]
    another operation x61 -> x0, matrix products: 120 us -> none  [the longest x30 93.6 us: shrink_factor(): return jnp.linalg.cholesky(weight)]
    gather x12 -> x0, local copies, waits for them, and re-layouts: 91.8 us -> none  [the longest x1 34.1 us: per_device(): log_all = jnp.log(jnp.diagonal(lower))]
    another operation x68 -> x0, local copies, waits for them, and re-layouts: 56.8 us -> none
    all_to_all x0 -> x2, blocking collectives: none -> 41.1 us  [the longest x1 22.7 us: per_device(): lax.all_to_all(send, ('ser', 'org'), split_axis=0, concat_axis=0, tiled=T...]
    pallas_call x0 -> x3, Pallas kernels: none -> 25.3 us  [the longest x1 19.3 us: per_device(): pl.pallas_call(functools.partial(owner_body, n_ser=n_ser, n_org=n_org, se...]
    div x1 -> x0, other arithmetic: 22.9 us -> none  [shrink_factor(): return jnp.linalg.cholesky(weight)]
  transfers between devices with their start and end apart: 2 -> 0, of which waited for: 0 -> 0; matrix products, arithmetic and copies ran while one was open for 8% -> 0% of each run, Pallas kernels for 0% -> 0%
where the time goes in v1:
time: 69.7 us; the launch traced here: 69.3 us
  blocking collectives  41.1 us (59%)
  Pallas kernels  25.3 us (36%)
  local copies, waits for them, and re-layouts  2.28 us (3%)
    all_to_all x1, blocking collectives, per_device(): lax.all_to_all(send, ('ser', 'org'), split_axis=0, concat_axis=0, tiled=T...  22.7 us
    pallas_call x1, Pallas kernels, per_device(): pl.pallas_call(functools.partial(owner_body, n_ser=n_ser, n_org=n_org, se...  19.3 us
    all_to_all x1, blocking collectives, per_device(): lax.all_to_all(back, ('ser', 'org'), split_axis=0, concat_axis=0, tiled=T...  18.4 us
    pallas_call x1, Pallas kernels, per_device(): pl.pallas_call(functools.partial(pack_body, n_ser=n_ser, n_org=n_org), ou...  4.63 us
    unnamed x10, local copies, waits for them, and re-layouts  2.28 us
    pallas_call x1, Pallas kernels, per_device(): pl.pallas_call(functools.partial(home_body, n_ser=n_ser, n_org=n_org), ou...  1.41 us

profile of v1, /device:TPU:0, one launch (start us, length us, event | category | flops | bytes accessed | tf_op | source)
XLA Modules:
  0.0 69.3 jit_solution(8762268162801447322)
XLA Ops:
  0.6 0.0 copy-start.4
  0.6 0.0 copy-start.3
  0.6 0.6 copy-done.4
  1.3 0.0 copy-done.3
  1.3 0.0 copy-start
  1.3 0.8 %copy-done = s32[8192]{0:T(1024)S(1)} copy-done((s32[8192]{0:T(1024)S(1)}, s32[8192]{0:T(1024)}, u32[]{:S(2)}) %copy-start) | copy-done | bytes 32792
  2.1 0.0 copy-start.2
  2.1 0.8 %copy-done.2 = f32[16,1024]{1,0:T(8,128)S(1)} copy-done((f32[16,1024]{1,0:T(8,128)S(1)}, f32[16,1024]{1,0:T(8,128)}, u32[]{:S(2)}) %copy-start.2) | copy-done | bytes 65560
  2.9 4.6 %pack.1 = (f32[32,16,256]{2,1,0:T(8,128)S(1)}, s32[8,128]{1,0:T(8,128)S(1)}) custom-call(s32[16]{0:T(128)S(1)} %copy-done.3, s32[16]{0:T(128)S(1)} %copy-done.4, f32[16,1024]{1,0:T(8,128)S(1)} %copy-done.2, s32[64,128]{1,0:T(8,128)S(1)} %bitcast.1), custom_call_target="tpu_custom_call" | custom-call | tf_op jit(solution)/shard_map/pack/pallas_call | solution.py:414
  7.5 0.0 copy-start.1
  7.6 22.7 %all_to_all.10.recv_ref = f32[32,16,256]{2,1,0:T(8,128)S(1)} all-to-all(f32[32,16,256]{2,1,0:T(8,128)S(1)} %get-tuple-element.6), channel_id=1, replica_groups=mesh['ser'=8,'org'=4] {'ser','org'}, dimensions={0} | all-to-all | bytes 1048576 | tf_op jit(solution)/shard_map/all_to_all | solution.py:423
  30.2 0.0 copy-done.1
  30.2 19.3 %owner.1 = (f32[32,16,256]{2,1,0:T(8,128)S(1)}, f32[1,512]{1,0:T(1,128)}) custom-call(s32[16]{0:T(128)S(1)} %copy-done.3, s32[16]{0:T(128)S(1)} %copy-done.4, f32[32,16,256]{2,1,0:T(8,128)S(1)} %all_to_all.10.recv_ref, s32[64,128]{1,0:T(8,128)S(1)} %bitcast.2), custom_call_target="tpu_custom_call" | custom-call | tf_op jit(solution)/shard_map/owner/pallas_call | solution.py:424
  49.5 18.4 %all_to_all.11.back_ref = f32[32,16,256]{2,1,0:T(8,128)S(1)} all-to-all(f32[32,16,256]{2,1,0:T(8,128)S(1)} %get-tuple-element.7), channel_id=1, replica_groups=mesh['ser'=8,'org'=4] {'ser','org'}, dimensions={0} | all-to-all | bytes 1048576 | tf_op jit(solution)/shard_map/all_to_all | solution.py:439
  67.9 1.4 %home.1 = f32[16,1024]{1,0:T(8,128)} custom-call(f32[32,16,256]{2,1,0:T(8,128)S(1)} %all_to_all.11.back_ref, s32[8,128]{1,0:T(8,128)S(1)} %get-tuple-element.8.dest_ref), custom_call_target="tpu_custom_call" | custom-call | tf_op jit(solution)/shard_map/home/pallas_call | solution.py:440
Async XLA Ops:
  0.6 0.7 copy-start.4
  0.6 0.7 copy-start.3
  1.3 0.8 %copy-start = (s32[8192]{0:T(1024)S(1)}, s32[8192]{0:T(1024)}, u32[]{:S(2)}) copy-start(s32[8192]{0:T(1024)} %param.7) | copy-start | bytes 98308
  2.1 0.8 %copy-start.2 = (f32[16,1024]{1,0:T(8,128)S(1)}, f32[16,1024]{1,0:T(8,128)}, u32[]{:S(2)}) copy-start(f32[16,1024]{1,0:T(8,128)} %x_ref.1) | copy-start | bytes 196612
  7.5 22.7 %copy-start.1 = (s32[8192]{0:T(1024)S(1)}, s32[8192]{0:T(1024)}, u32[]{:S(2)}) copy-start(s32[8192]{0:T(1024)} %param.7) | copy-start | bytes 98308

commit v2 on v1

--- a/solution.py
+++ b/solution.py
@@ -13,6 +13,8 @@
 ROWS = TILE // LANES
 BLOCK = 64
 OWNER_TILES = SLOTS // TILE
+PANEL = 16
+PIVOTS = 8
 
 epsilon = 1e-06
 
@@ -56,8 +58,37 @@
 
 
 def pack_body(
-    size_ref, owner_ref, x_ref, perm_ref, send_ref, dest_ref, place_ref, *, n_ser, n_org
+    size_hbm,
+    owner_hbm,
+    x_hbm,
+    perm_hbm,
+    send_hbm,
+    dest_ref,
+    size_ref,
+    owner_ref,
+    x_ref,
+    perm_ref,
+    place_ref,
+    send_ref,
+    in_sems,
+    out_sems,
+    *,
+    n_ser,
+    n_org,
 ):
+    loads = [
+        pltpu.make_async_copy(source, target, in_sems.at[i])
+        for i, (source, target) in enumerate(
+            [
+                (size_hbm, size_ref),
+                (owner_hbm, owner_ref),
+                (perm_hbm, perm_ref),
+                (x_hbm, x_ref),
+            ]
+        )
+    ]
+    for load in loads:
+        load.start()
     here = lax.axis_index("ser")
     n_sub = size_ref.shape[0]
     rows = perm_ref.shape[0]
@@ -65,6 +96,8 @@
     per_peer = SLOTS // n_ser
     shift = ser_dev.bit_length() - 1
     groups = ser_dev // LANES
+    for load in loads[:3]:
+        load.wait()
 
     def owner_of(row_ids):
         owner = jnp.zeros(row_ids.shape, jnp.int32)
@@ -109,20 +142,39 @@
             jnp.concatenate(lefts, axis=1), jnp.concatenate(rights, axis=1), NT
         )
 
-    found = lax.fori_loop(0, rows // 8, to_local, jnp.zeros((2 * groups, LANES), jnp.float32))
+    steps = rows // 8
+    found = lax.fori_loop(
+        0,
+        steps,
+        to_local,
+        jnp.zeros((2 * groups, LANES), jnp.float32),
+        unroll=steps <= 8,
+    )
     dest = (found[:groups] * 16.0 + found[groups:]).astype(jnp.int32)
     dest_ref[...] = dest
+    loads[3].wait()
     terms = split_three(x_ref[...])
+
+    def store(o, r):
+        return pltpu.make_async_copy(
+            send_ref.at[o], send_hbm.at[o * n_org + r], out_sems.at[o * n_org + r]
+        )
 
     def pack(o, carry):
         target = iota((per_peer, LANES), 0) + o * per_peer
         pick = jnp.concatenate([as_bf16(target == dest[h : h + 1]) for h in range(groups)], axis=1)
-        columns = join_three(dot_bf16(terms, pick, NT))
+        send_ref[o] = join_three(dot_bf16(terms, pick, NT))
         for r in range(n_org):
-            send_ref[o * n_org + r] = columns
+            store(o, r).start()
         return carry
 
-    lax.fori_loop(0, n_ser, pack, 0)
+    def finish(o, carry):
+        for r in range(n_org):
+            store(o, r).wait()
+        return carry
+
+    lax.fori_loop(0, n_ser, pack, 0, unroll=n_ser <= 8)
+    lax.fori_loop(0, n_ser, finish, 0, unroll=n_ser <= 8)
 
 
 def lane_pick(value, index):
@@ -132,65 +184,100 @@
 def eliminate(parts, size, whole):
     lane = iota((8, LANES), 1)
     sub = iota((8, LANES), 0)
-    shift = lane & (LANES - size)
+    base = lane & (LANES - size)
+    local = lane & (size - 1)
     parts = [list(part) for part in parts]
     downs = [[jnp.ones((8, LANES), jnp.float32)] * len(part) for part in parts]
     acrosses = [jnp.ones((8, LANES), jnp.float32) for _ in parts]
-    for j in range(0, size, 2):
-        g, s = divmod(j, 8)
-        column0 = shift + j
-        column1 = shift + (j + 1)
-        on0, on1 = lane == column0, lane == column1
-        on = on0 | on1
+    tall = PANEL // 8
+    count = PIVOTS
+    for top in range(0, size, PANEL):
+        first = top // 8
+        inside = (local >= top) & (local < top + PANEL)
+        panels = [part[first : first + tall] for part in parts]
+        kept = [list(panel) for panel in panels]
+        for j in range(top, top + PANEL, count):
+            g, s = divmod(j - top, 8)
+            columns = [base + (j + a) for a in range(count)]
+            at = [local == j + a for a in range(count)]
+            on = (local >= j) & (local < j + count)
+            for p, panel in enumerate(panels):
+                picked = [[lane_pick(piece, column) for column in columns] for piece in panel]
+                corner = [
+                    [
+                        jnp.broadcast_to(picked[g][b][s + a : s + a + 1], (8, LANES))
+                        for b in range(a + 1)
+                    ]
+                    for a in range(count)
+                ]
+                inv, low = [], [[None] * count for _ in range(count)]
+                for k in range(count):
+                    inv.append(1.0 / corner[k][k])
+                    for a in range(k + 1, count):
+                        low[a][k] = corner[a][k] * inv[k]
+                    for a in range(k + 1, count):
+                        for b in range(k + 1, a + 1):
+                            corner[a][b] = corner[a][b] - low[a][k] * corner[b][k]
+                rows, solved = [], [None] * count
+                for a in range(count):
+                    row = jnp.broadcast_to(panel[g][s + a : s + a + 1], (8, LANES))
+                    row = jnp.where(on, jnp.where(at[a], 1.0, 0.0), row)
+                    for b in range(a):
+                        row = row - low[a][b] * rows[b]
+                    rows.append(row)
+                for a in reversed(range(count)):
+                    row = rows[a] * inv[a]
+                    for b in range(a + 1, count):
+                        row = row - low[b][a] * solved[b]
+                    solved[a] = row
+                for v in range(tall):
+                    new = jnp.where(on, 0.0, panel[v])
+                    for a in range(count):
+                        new = new - picked[v][a] * solved[a]
+                    if v == g:
+                        for a in range(count):
+                            new = jnp.where(sub == s + a, solved[a], new)
+                    panel[v] = new
+                if not whole:
+                    for v in range(g, tall):
+                        ahead = (sub >= s + count) | (v > g)
+                        kept[p][v] = jnp.where(ahead, panel[v], kept[p][v])
+                    for a in range(count):
+                        here = sub == s + a
+                        pivot = corner[a][a]
+                        kept[p][g] = jnp.where(here, rows[a], kept[p][g])
+                        downs[p][first + g] = jnp.where(here, pivot, downs[p][first + g])
+                        acrosses[p] = jnp.where(at[a], pivot, acrosses[p])
         for p, part in enumerate(parts):
-            row0 = jnp.broadcast_to(part[g][s : s + 1], (8, LANES))
-            row1 = jnp.broadcast_to(part[g][s + 1 : s + 2], (8, LANES))
-            first = lane_pick(row0, column0)
-            cross = lane_pick(row0, column1)
-            second = lane_pick(row1, column1)
-            row0 = jnp.where(on, jnp.where(on0, 1.0, 0.0), row0)
-            row1 = jnp.where(on, jnp.where(on1, 1.0, 0.0), row1)
-            inv = 1.0 / first
-            step = cross * inv
-            pivot = second - step * cross
-            inv1 = 1.0 / pivot
-            next1 = row1 - step * row0
-            solved1 = next1 * inv1
-            solved0 = row0 * inv - step * solved1
-            for i in range(0 if whole else g, len(part)):
-                old = part[i]
-                new = (
-                    jnp.where(on, 0.0, old)
-                    - lane_pick(old, column0) * solved0
-                    - lane_pick(old, column1) * solved1
+            others = [i for i in range(len(part)) if i >= first + tall or (whole and i < first)]
+            if others:
+                zero = jnp.zeros((8, LANES), jnp.float32)
+                pieces = []
+                for h in range(LANES // size):
+                    half = base == h * size
+                    for i in range(size // 8):
+                        if first <= i < first + tall:
+                            pieces.append(jnp.where(half, panels[p][i - first], 0.0))
+                        else:
+                            pieces.append(zero)
+                change = dot_f32(
+                    jnp.concatenate([part[i] for i in others], axis=0),
+                    jnp.concatenate(pieces, axis=0),
                 )
-                if i == g:
-                    if whole:
-                        new = jnp.where(sub == s, solved0, jnp.where(sub == s + 1, solved1, new))
-                    else:
-                        new = jnp.where(sub <= s, old, jnp.where(sub == s + 1, next1, new))
-                        new = jnp.where(sub == s, row0, new)
-                part[i] = new
-            if not whole:
-                downs[p][g] = jnp.where(
-                    sub == s, first, jnp.where(sub == s + 1, pivot, downs[p][g])
-                )
-                acrosses[p] = jnp.where(on0, first, jnp.where(on1, pivot, acrosses[p]))
+                for n, i in enumerate(others):
+                    part[i] = jnp.where(inside, 0.0, part[i]) - change[n * 8 : n * 8 + 8]
+            part[first : first + tall] = panels[p] if whole else kept[p]
     return parts, downs, acrosses
 
 
-def owner_body(
+def slots_body(
     size_ref,
     owner_ref,
-    recv_ref,
     perm_ref,
-    back_ref,
-    log_ref,
-    all_ref,
+    pick_ref,
+    tile_of_ref,
+    tile_ref,
     index_ref,
-    pick_ref,
-    inverse_ref,
-    tile_ref,
     *,
     n_ser,
     n_org,
@@ -199,8 +286,6 @@
     here = lax.axis_index("ser")
     part = lax.axis_index("org")
     n_sub = size_ref.shape[0]
-    t_dev = recv_ref.shape[1]
-    anchors = t_dev * n_org
     per_peer = SLOTS // n_ser
     share = SLOTS // n_org
     tiles = share // TILE
@@ -227,12 +312,6 @@
         lax.fori_loop(0, held, put, 0)
         at = at + held
         first = first + count
-
-    for d in range(n_ser):
-        for r in range(n_org):
-            all_ref[r * t_dev : (r + 1) * t_dev, d * per_peer : (d + 1) * per_peer] = recv_ref[
-                d * n_org + r
-            ]
 
     pieces = []
     for t in range(OWNER_TILES):
@@ -264,6 +343,40 @@
             jnp.int32
         )
     tile_of = jnp.concatenate([tile_of[d : d + 1] for d in range(n_ser)], axis=1)
+    tile_of_ref[...] = tile_of
+
+    for i in range(share // LANES):
+        row = index_ref[pl.ds(part * (tiles * ROWS) + i, 1), :]
+        pick_ref[:, i * LANES : (i + 1) * LANES] = as_bf16(iota((SLOTS, LANES), 0) == row)
+
+
+def owner_body(
+    recv_ref,
+    pick_ref,
+    tile_of_ref,
+    tile_ref,
+    back_ref,
+    log_ref,
+    all_ref,
+    inverse_ref,
+    *,
+    n_ser,
+    n_org,
+):
+    part = lax.axis_index("org")
+    t_dev = recv_ref.shape[1]
+    anchors = t_dev * n_org
+    per_peer = SLOTS // n_ser
+    share = SLOTS // n_org
+    tiles = share // TILE
+
+    for d in range(n_ser):
+        for r in range(n_org):
+            all_ref[r * t_dev : (r + 1) * t_dev, d * per_peer : (d + 1) * per_peer] = recv_ref[
+                d * n_org + r
+            ]
+
+    tile_of = tile_of_ref[...]
 
     block = all_ref[...]
     spread = jnp.sum(block * block, axis=0, keepdims=True) * (1.0 / anchors)
@@ -277,19 +390,27 @@
         filled.append(tile_ref[0, t] >= 0)
         in_tree.append((tile_of >= low) & (tile_of < high))
         ahead_of.append((tile_of >= low) & (tile_of < t))
-    grams = dot_f32(
+    terms = split_three(scaled)
+    weighted = split_three(scaled * own)
+    products = dot_bf16(
         jnp.concatenate(
-            [scaled * jnp.where(mask, own, 0.0) for mask in in_tree]
-            + [jnp.where(mask, scaled, 0.0) for mask in ahead_of],
+            [weighted * as_bf16(mask) for mask in in_tree]
+            + [terms * as_bf16(mask) for mask in ahead_of],
             axis=0,
         ),
-        scaled,
+        terms,
         NT,
     )
+    grams = []
+    for u in range(2 * tiles):
+        piece = join_three(products[u * 3 * anchors : (u + 1) * 3 * anchors])
+        grams.append(
+            piece[:, 2 * anchors :] + piece[:, anchors : 2 * anchors] + piece[:, :anchors]
+        )
     unit = iota((anchors, anchors), 0) == iota((anchors, anchors), 1)
     shrink = []
     for u in range(tiles):
-        dual = grams[u * anchors : (u + 1) * anchors] * (1.0 / anchors)
+        dual = grams[u] * (1.0 / anchors)
         own_square = jnp.where(in_tree[u], own * own, 0.0)
         square = dual * dual
         total = lambda value: jnp.sum(
@@ -300,12 +421,10 @@
         upper = (upper - lower) / (anchors - 1)
         shrink.append(jnp.where(filled[u], jnp.minimum(upper / jnp.where(filled[u], lower, 1.0), 1.0), 1.0))
 
-    for i in range(share // LANES):
-        row = index_ref[pl.ds(part * (tiles * ROWS) + i, 1), :]
-        pick_ref[:, i * LANES : (i + 1) * LANES] = as_bf16(iota((SLOTS, LANES), 0) == row)
-    mine = join_three(dot_bf16(split_three(block), pick_ref[...]))
-    my_spread = jnp.sum(mine * mine, axis=0, keepdims=True) * (1.0 / anchors)
-    mine = mine * jnp.where(my_spread > 0, lax.rsqrt(my_spread), 0.0)
+    levels = split_three(jnp.broadcast_to(spread, (16, SLOTS)))
+    found = dot_bf16(jnp.concatenate([terms, levels], axis=0), pick_ref[...])
+    mine = join_three(found[: 3 * anchors])
+    my_spread = join_three(found[3 * anchors :])[:1]
     mine_down = mine.T
 
     per_tile = TILE // BLOCK
@@ -313,7 +432,7 @@
     side = LANES // anchors
     rows_of = lambda b: slice(b * BLOCK, (b + 1) * BLOCK)
     for u in range(tiles):
-        prior = grams[(tiles + u) * anchors : (tiles + u + 1) * anchors]
+        prior = grams[tiles + u]
         gain = (1.0 - shrink[u]) * (1.0 / anchors)
         for v in range(per_tile):
             b = u * per_tile + v
@@ -406,36 +525,60 @@
     blocks = share // BLOCK
     side = LANES // anchors
     perm = series_perm.reshape(-1, LANES)
+    to_hbm = lambda value: pltpu.with_memory_space_constraint(value, pltpu.HBM)
     vmem = pl.BlockSpec(memory_space=pltpu.VMEM)
     smem = pl.BlockSpec(memory_space=pltpu.SMEM)
+    hbm = pl.BlockSpec(memory_space=pltpu.HBM)
     params = pltpu.CompilerParams(vmem_limit_bytes=48 * 1024 * 1024)
     blocks_shape = jax.ShapeDtypeStruct((n_ser * n_org, t_dev, per_peer), jnp.float32)
 
     send, dest = pl.pallas_call(
         functools.partial(pack_body, n_ser=n_ser, n_org=n_org),
         out_shape=(blocks_shape, jax.ShapeDtypeStruct((ser_dev // LANES, LANES), jnp.int32)),
-        in_specs=[smem, smem, vmem, vmem],
-        out_specs=(vmem, vmem),
-        scratch_shapes=[pltpu.VMEM(perm.shape, jnp.int32)],
+        in_specs=[hbm, hbm, hbm, hbm],
+        out_specs=(hbm, vmem),
+        scratch_shapes=[
+            pltpu.SMEM(sub_size.shape, jnp.int32),
+            pltpu.SMEM(sub_owner.shape, jnp.int32),
+            pltpu.VMEM(residual.shape, jnp.float32),
+            pltpu.VMEM(perm.shape, jnp.int32),
+            pltpu.VMEM(perm.shape, jnp.int32),
+            pltpu.VMEM((n_ser, t_dev, per_peer), jnp.float32),
+            pltpu.SemaphoreType.DMA((4,)),
+            pltpu.SemaphoreType.DMA((n_ser * n_org,)),
+        ],
         compiler_params=params,
         name="pack",
-    )(sub_size, sub_owner, residual, perm)
+    )(to_hbm(sub_size), to_hbm(sub_owner), to_hbm(residual), to_hbm(perm))
     recv = lax.all_to_all(send, ("ser", "org"), split_axis=0, concat_axis=0, tiled=True)
+    pick, tile_of, tile = pl.pallas_call(
+        functools.partial(slots_body, n_ser=n_ser, n_org=n_org, ser_dev=ser_dev),
+        out_shape=(
+            jax.ShapeDtypeStruct((SLOTS, share), jnp.bfloat16),
+            jax.ShapeDtypeStruct((1, SLOTS), jnp.int32),
+            jax.ShapeDtypeStruct((3, OWNER_TILES), jnp.int32),
+        ),
+        in_specs=[smem, smem, vmem],
+        out_specs=(vmem, vmem, smem),
+        scratch_shapes=[pltpu.VMEM((SLOTS // LANES, LANES), jnp.int32)],
+        compiler_params=params,
+        cost_estimate=pl.CostEstimate(
+            flops=4_000_000_000, bytes_accessed=4_000_000, transcendentals=0
+        ),
+        name="slots",
+    )(sub_size, sub_owner, perm)
     back, log_part = pl.pallas_call(
-        functools.partial(owner_body, n_ser=n_ser, n_org=n_org, ser_dev=ser_dev),
+        functools.partial(owner_body, n_ser=n_ser, n_org=n_org),
         out_shape=(blocks_shape, jax.ShapeDtypeStruct((1, share), jnp.float32)),
-        in_specs=[smem, smem, vmem, vmem],
+        in_specs=[vmem, vmem, vmem, smem],
         out_specs=(vmem, vmem),
         scratch_shapes=[
             pltpu.VMEM((anchors, SLOTS), jnp.float32),
-            pltpu.VMEM((SLOTS // LANES, LANES), jnp.int32),
-            pltpu.VMEM((SLOTS, share), jnp.bfloat16),
             pltpu.VMEM((blocks // side, anchors, LANES), jnp.float32),
-            pltpu.SMEM((3, OWNER_TILES), jnp.int32),
         ],
         compiler_params=params,
         name="owner",
-    )(sub_size, sub_owner, recv, perm)
+    )(recv, pick, tile_of, tile)
     returned = lax.all_to_all(back, ("ser", "org"), split_axis=0, concat_axis=0, tiled=True)
     whitened = pl.pallas_call(
         functools.partial(home_body, n_ser=n_ser, n_org=n_org),

time: 69.7 us -> 57.8 us (0.83)
  blocking collectives: 41.1 us -> 18.4 us
  waiting for transfers between devices: 0 us -> 11.4 us
  Pallas kernels: 25.3 us -> 17.6 us
  starting transfers between devices: 0 us -> 7.3 us
    all_to_all x1 -> x0, blocking collectives: 22.7 us -> none  [per_device(): lax.all_to_all(send, ('ser', 'org'), split_axis=0, concat_axis=0, tiled=T...]
    all_to_all x0 -> x1, waiting for transfers between devices: none -> 11.4 us  [per_device(): lax.all_to_all(send, ('ser', 'org'), split_axis=0, concat_axis=0, tiled=T...]
    all_to_all x0 -> x1, starting transfers between devices: none -> 7.3 us  [per_device(): lax.all_to_all(send, ('ser', 'org'), split_axis=0, concat_axis=0, tiled=T...]
    pallas_call x1 -> x2, Pallas kernels: 19.3 us -> 12.2 us  [the longest x1 10.2 us: per_device(): pl.pallas_call(functools.partial(owner_body, n_ser=n_ser, n_org=n_org), o...]
    unnamed x10 -> x6, local copies, waits for them, and re-layouts: 2.28 us -> 2.06 us
  transfers between devices with their start and end apart: 0 -> 1, of which waited for: 0 -> 1; matrix products, arithmetic and copies ran while one was open for 0% -> 0% of each run, Pallas kernels for 0% -> 4%
where the time goes in v2:
time: 57.8 us; the launch traced here: 57.5 us
  blocking collectives  18.4 us (32%)
  Pallas kernels  17.6 us (30%)
  waiting for transfers between devices  11.4 us (20%)
  starting transfers between devices  7.3 us (13%)
  local copies, waits for them, and re-layouts  2.06 us (4%)
  between operations  0.67 us (1%)
    all_to_all x1, blocking collectives, per_device(): lax.all_to_all(back, ('ser', 'org'), split_axis=0, concat_axis=0, tiled=T...  18.4 us
    all_to_all x1, waiting for transfers between devices, per_device(): lax.all_to_all(send, ('ser', 'org'), split_axis=0, concat_axis=0, tiled=T...  11.4 us
    pallas_call x1, Pallas kernels, per_device(): pl.pallas_call(functools.partial(owner_body, n_ser=n_ser, n_org=n_org), o...  10.2 us
    all_to_all x1, starting transfers between devices, per_device(): lax.all_to_all(send, ('ser', 'org'), split_axis=0, concat_axis=0, tiled=T...  7.3 us
    pallas_call x1, Pallas kernels, per_device(): pl.pallas_call(functools.partial(pack_body, n_ser=n_ser, n_org=n_org), ou...  3.97 us
    pallas_call x1, Pallas kernels, per_device(): pl.pallas_call(functools.partial(slots_body, n_ser=n_ser, n_org=n_org, se...  2.08 us
    unnamed x6, local copies, waits for them, and re-layouts  2.06 us
    pallas_call x1, Pallas kernels, per_device(): pl.pallas_call(functools.partial(home_body, n_ser=n_ser, n_org=n_org), ou...  1.41 us
  transfers between devices with their start and end apart: 1, of which 1 were waited for; matrix products, arithmetic and copies ran while one was open for 0% of the time, Pallas kernels for 4%

profile of v2, /device:TPU:0, one launch (start us, length us, event | category | flops | bytes accessed | tf_op | source)
XLA Modules:
  0.0 57.5 jit_solution(16380233192442068313)
XLA Ops:
  0.6 4.0 %pack.1 = (f32[32,16,256]{2,1,0:T(8,128)}, s32[8,128]{1,0:T(8,128)S(1)}) custom-call(s32[16]{0:T(128)} %size_ref.1, s32[16]{0:T(128)} %owner_ref.1, f32[16,1024]{1,0:T(8,128)} %x_hbm.1, s32[64,128]{1,0:T(8,128)} %bitcast.1), custom_call_target="tpu_custom_call" | custom-call | tf_op jit(solution)/shard_map/pack/pallas_call | solution.py:535
  4.6 7.3 %all-to-all-start = ((f32[32,16,256]{2,1,0:T(8,128)}), f32[32,16,256]{2,1,0:T(8,128)S(1)}, u32[]{:S(2)}, u32[]{:S(2)}) async-start(f32[32,16,256]{2,1,0:T(8,128)} %get-tuple-element.9), calls=%async_computation | async-start | bytes 1048576 | tf_op jit(solution)/shard_map/all_to_all | solution.py:553
  11.9 0.0 copy-start
  11.9 0.7 %copy-done = s32[8192]{0:T(1024)S(1)} copy-done((s32[8192]{0:T(1024)S(1)}, s32[8192]{0:T(1024)}, u32[]{:S(2)}) %copy-start) | copy-done | bytes 32792
  12.7 0.0 copy-start.1
  12.7 0.7 %copy-done.1 = s32[16]{0:T(128)S(1)} copy-done((s32[16]{0:T(128)S(1)}, s32[16]{0:T(128)}, u32[]{:S(2)}) %copy-start.1) | copy-done | bytes 88
  13.3 0.0 copy-start.2
  13.3 0.7 %copy-done.2 = s32[16]{0:T(128)S(1)} copy-done((s32[16]{0:T(128)S(1)}, s32[16]{0:T(128)}, u32[]{:S(2)}) %copy-start.2) | copy-done | bytes 88
  14.0 2.1 %slots.1 = (bf16[2048,512]{1,0:T(8,128)(2,1)S(1)}, s32[1,2048]{1,0:T(1,128)S(1)}, s32[3,8]{1,0:T(4,128)S(1)}) custom-call(s32[16]{0:T(128)S(1)} %copy-done.1, s32[16]{0:T(128)S(1)} %copy-done.2, s32[64,128]{1,0:T(8,128)S(1)} %bitcast.2), custom_call_target="tpu_custom_call" | custom-call | flops 4000000000 | bytes 4000000 | tf_op jit(solution)/shard_map/slots/pallas_call | solution.py:554
  16.1 11.4 %all-to-all-done.recv_ref = f32[32,16,256]{2,1,0:T(8,128)S(1)} async-done(((f32[32,16,256]{2,1,0:T(8,128)}), f32[32,16,256]{2,1,0:T(8,128)S(1)}, u32[]{:S(2)}, u32[]{:S(2)}) %all-to-all-start) | async-done | bytes 524320 | tf_op jit(solution)/shard_map/all_to_all | solution.py:553
  27.5 10.2 %owner.1 = (f32[32,16,256]{2,1,0:T(8,128)S(1)}, f32[1,512]{1,0:T(1,128)}) custom-call(f32[32,16,256]{2,1,0:T(8,128)S(1)} %all-to-all-done.recv_ref, bf16[2048,512]{1,0:T(8,128)(2,1)S(1)} %get-tuple-element.10.pick_ref, s32[1,2048]{1,0:T(1,128)S(1)} %get-tuple-element.11.tile_of_ref, s32[3,8]{1,0:T(4,128)S(1)} %get-tuple-element.12.tile_ref), custom_call_target="tpu_custom_call" | custom-call | tf_op jit(solution)/shard_map/owner/pallas_call | solution.py:570
  37.6 18.4 %all_to_all.10.back_ref = f32[32,16,256]{2,1,0:T(8,128)S(1)} all-to-all(f32[32,16,256]{2,1,0:T(8,128)S(1)} %get-tuple-element.13), channel_id=1, replica_groups=mesh['ser'=8,'org'=4] {'ser','org'}, dimensions={0} | all-to-all | bytes 1048576 | tf_op jit(solution)/shard_map/all_to_all | solution.py:582
  56.1 1.4 %home.1 = f32[16,1024]{1,0:T(8,128)} custom-call(f32[32,16,256]{2,1,0:T(8,128)S(1)} %all_to_all.10.back_ref, s32[8,128]{1,0:T(8,128)S(1)} %get-tuple-element.14.dest_ref), custom_call_target="tpu_custom_call" | custom-call | tf_op jit(solution)/shard_map/home/pallas_call | solution.py:583
Async XLA Ops:
  4.6 22.9 %all-to-all-start = ((f32[32,16,256]{2,1,0:T(8,128)}), f32[32,16,256]{2,1,0:T(8,128)S(1)}, u32[]{:S(2)}, u32[]{:S(2)}) async-start(f32[32,16,256]{2,1,0:T(8,128)} %get-tuple-element.9), calls=%async_computation | async-start | bytes 1048576 | tf_op jit(solution)/shard_map/all_to_all | solution.py:553
  11.9 0.8 %copy-start = (s32[8192]{0:T(1024)S(1)}, s32[8192]{0:T(1024)}, u32[]{:S(2)}) copy-start(s32[8192]{0:T(1024)} %param.7) | copy-start | bytes 98308
  12.7 0.7 %copy-start.1 = (s32[16]{0:T(128)S(1)}, s32[16]{0:T(128)}, u32[]{:S(2)}) copy-start(s32[16]{0:T(128)} %size_ref.1) | copy-start | bytes 196
  13.3 0.7 %copy-start.2 = (s32[16]{0:T(128)S(1)}, s32[16]{0:T(128)}, u32[]{:S(2)}) copy-start(s32[16]{0:T(128)} %owner_ref.1) | copy-start | bytes 196

commit v3 on v2

--- a/solution.py
+++ b/solution.py
@@ -157,20 +157,18 @@
 
     def store(o, r):
         return pltpu.make_async_copy(
-            send_ref.at[o], send_hbm.at[o * n_org + r], out_sems.at[o * n_org + r]
+            send_ref.at[o], send_hbm.at[o], out_sems.at[o]
         )
 
     def pack(o, carry):
         target = iota((per_peer, LANES), 0) + o * per_peer
         pick = jnp.concatenate([as_bf16(target == dest[h : h + 1]) for h in range(groups)], axis=1)
         send_ref[o] = join_three(dot_bf16(terms, pick, NT))
-        for r in range(n_org):
-            store(o, r).start()
+        store(o, 0).start()
         return carry
 
     def finish(o, carry):
-        for r in range(n_org):
-            store(o, r).wait()
+        store(o, 0).wait()
         return carry
 
     lax.fori_loop(0, n_ser, pack, 0, unroll=n_ser <= 8)
@@ -373,7 +371,7 @@
     for d in range(n_ser):
         for r in range(n_org):
             all_ref[r * t_dev : (r + 1) * t_dev, d * per_peer : (d + 1) * per_peer] = recv_ref[
-                d * n_org + r
+                r * n_ser + d
             ]
 
     tile_of = tile_of_ref[...]
@@ -534,7 +532,7 @@
 
     send, dest = pl.pallas_call(
         functools.partial(pack_body, n_ser=n_ser, n_org=n_org),
-        out_shape=(blocks_shape, jax.ShapeDtypeStruct((ser_dev // LANES, LANES), jnp.int32)),
+        out_shape=(jax.ShapeDtypeStruct((n_ser, t_dev, per_peer), jnp.float32), jax.ShapeDtypeStruct((ser_dev // LANES, LANES), jnp.int32)),
         in_specs=[hbm, hbm, hbm, hbm],
         out_specs=(hbm, vmem),
         scratch_shapes=[
@@ -550,7 +548,8 @@
         compiler_params=params,
         name="pack",
     )(to_hbm(sub_size), to_hbm(sub_owner), to_hbm(residual), to_hbm(perm))
-    recv = lax.all_to_all(send, ("ser", "org"), split_axis=0, concat_axis=0, tiled=True)
+    recv = lax.all_to_all(send, "ser", split_axis=0, concat_axis=0, tiled=True)
+    recv = lax.all_gather(recv, "org", axis=0, tiled=True)
     pick, tile_of, tile = pl.pallas_call(
         functools.partial(slots_body, n_ser=n_ser, n_org=n_org, ser_dev=ser_dev),
         out_shape=(

time: 57.8 us -> 55.9 us (0.967)
  waiting for transfers between devices: 11.4 us -> 3.18 us
  blocking collectives: 18.4 us -> 24.7 us
    all_to_all x1, waiting for transfers between devices: 11.4 us -> 3.18 us  [per_device(): recv = lax.all_to_all(send, 'ser', split_axis=0, concat_axis=0, tiled=True)]
    all_gather x0 -> x1, blocking collectives: none -> 7.15 us  [per_device(): recv = lax.all_gather(recv, 'org', axis=0, tiled=True)]
    all_to_all x1, blocking collectives: 18.4 us -> 17.6 us  [per_device(): lax.all_to_all(back, ('ser', 'org'), split_axis=0, concat_axis=0, tiled=T...]
where the time goes in v3:
time: 55.9 us; the launch traced here: 55.5 us
  blocking collectives  24.7 us (44%)
  Pallas kernels  17.6 us (31%)
  starting transfers between devices  7.29 us (13%)
  waiting for transfers between devices  3.18 us (6%)
  local copies, waits for them, and re-layouts  2.06 us (4%)
  between operations  0.66 us (1%)
    all_to_all x1, blocking collectives, per_device(): lax.all_to_all(back, ('ser', 'org'), split_axis=0, concat_axis=0, tiled=T...  17.6 us
    pallas_call x1, Pallas kernels, per_device(): pl.pallas_call(functools.partial(owner_body, n_ser=n_ser, n_org=n_org), o...  10.2 us
    all_to_all x1, starting transfers between devices, per_device(): recv = lax.all_to_all(send, 'ser', split_axis=0, concat_axis=0, tiled=True)  7.29 us
    all_gather x1, blocking collectives, per_device(): recv = lax.all_gather(recv, 'org', axis=0, tiled=True)  7.15 us
    pallas_call x1, Pallas kernels, per_device(): pl.pallas_call(functools.partial(pack_body, n_ser=n_ser, n_org=n_org), ou...  3.93 us
    all_to_all x1, waiting for transfers between devices, per_device(): recv = lax.all_to_all(send, 'ser', split_axis=0, concat_axis=0, tiled=True)  3.18 us
    pallas_call x1, Pallas kernels, per_device(): pl.pallas_call(functools.partial(slots_body, n_ser=n_ser, n_org=n_org, se...  2.08 us
    unnamed x6, local copies, waits for them, and re-layouts  2.06 us
  transfers between devices with their start and end apart: 1, of which 1 were waited for; matrix products, arithmetic and copies ran while one was open for 0% of the time, Pallas kernels for 4%

profile of v3, /device:TPU:0, one launch (start us, length us, event | category | flops | bytes accessed | tf_op | source)
XLA Modules:
  0.0 55.5 jit_solution(5782051647874094880)
XLA Ops:
  0.6 3.9 %pack.1 = (f32[8,16,256]{2,1,0:T(8,128)}, s32[8,128]{1,0:T(8,128)S(1)}) custom-call(s32[16]{0:T(128)} %size_ref.1, s32[16]{0:T(128)} %owner_ref.1, f32[16,1024]{1,0:T(8,128)} %x_hbm.1, s32[64,128]{1,0:T(8,128)} %bitcast.1), custom_call_target="tpu_custom_call" | custom-call | tf_op jit(solution)/shard_map/pack/pallas_call | solution.py:533
  4.6 7.3 %all-to-all-start = ((f32[8,16,256]{2,1,0:T(8,128)}), f32[8,16,256]{2,1,0:T(8,128)S(1)}, u32[]{:S(2)}, u32[]{:S(2)}) async-start(f32[8,16,256]{2,1,0:T(8,128)} %get-tuple-element.9), calls=%async_computation | async-start | bytes 262144 | tf_op jit(solution)/shard_map/all_to_all | solution.py:551
  11.9 0.0 copy-start
  11.9 0.8 %copy-done = s32[8192]{0:T(1024)S(1)} copy-done((s32[8192]{0:T(1024)S(1)}, s32[8192]{0:T(1024)}, u32[]{:S(2)}) %copy-start) | copy-done | bytes 32792
  12.6 0.0 copy-start.1
  12.6 0.7 %copy-done.1 = s32[16]{0:T(128)S(1)} copy-done((s32[16]{0:T(128)S(1)}, s32[16]{0:T(128)}, u32[]{:S(2)}) %copy-start.1) | copy-done | bytes 88
  13.3 0.0 copy-start.2
  13.3 0.7 %copy-done.2 = s32[16]{0:T(128)S(1)} copy-done((s32[16]{0:T(128)S(1)}, s32[16]{0:T(128)}, u32[]{:S(2)}) %copy-start.2) | copy-done | bytes 88
  13.9 2.1 %slots.1 = (bf16[2048,512]{1,0:T(8,128)(2,1)S(1)}, s32[1,2048]{1,0:T(1,128)S(1)}, s32[3,8]{1,0:T(4,128)S(1)}) custom-call(s32[16]{0:T(128)S(1)} %copy-done.1, s32[16]{0:T(128)S(1)} %copy-done.2, s32[64,128]{1,0:T(8,128)S(1)} %bitcast.2), custom_call_target="tpu_custom_call" | custom-call | flops 4000000000 | bytes 4000000 | tf_op jit(solution)/shard_map/slots/pallas_call | solution.py:553
  16.0 3.2 %all-to-all-done = f32[8,16,256]{2,1,0:T(8,128)S(1)} async-done(((f32[8,16,256]{2,1,0:T(8,128)}), f32[8,16,256]{2,1,0:T(8,128)S(1)}, u32[]{:S(2)}, u32[]{:S(2)}) %all-to-all-start) | async-done | bytes 131104 | tf_op jit(solution)/shard_map/all_to_all | solution.py:551
  19.2 7.2 %all_gather.3.recv_ref = f32[32,16,256]{2,1,0:T(8,128)S(1)} all-gather(f32[8,16,256]{2,1,0:T(8,128)S(1)} %all-to-all-done), channel_id=1, replica_groups=mesh['ser'=8,'org'=4] {'org'}, dimensions={0}, use_global_device_ids=true | all-gather | bytes 655360 | tf_op jit(solution)/shard_map/all_gather | solution.py:552
  26.4 10.2 %owner.1 = (f32[32,16,256]{2,1,0:T(8,128)S(1)}, f32[1,512]{1,0:T(1,128)}) custom-call(f32[32,16,256]{2,1,0:T(8,128)S(1)} %all_gather.3.recv_ref, bf16[2048,512]{1,0:T(8,128)(2,1)S(1)} %get-tuple-element.10.pick_ref, s32[1,2048]{1,0:T(1,128)S(1)} %get-tuple-element.11.tile_of_ref, s32[3,8]{1,0:T(4,128)S(1)} %get-tuple-element.12.tile_ref), custom_call_target="tpu_custom_call" | custom-call | tf_op jit(solution)/shard_map/owner/pallas_call | solution.py:569
  36.5 17.6 %all_to_all.10.back_ref = f32[32,16,256]{2,1,0:T(8,128)S(1)} all-to-all(f32[32,16,256]{2,1,0:T(8,128)S(1)} %get-tuple-element.13), channel_id=1, replica_groups=mesh['ser'=8,'org'=4] {'ser','org'}, dimensions={0} | all-to-all | bytes 1048576 | tf_op jit(solution)/shard_map/all_to_all | solution.py:581
  54.1 1.4 %home.1 = f32[16,1024]{1,0:T(8,128)} custom-call(f32[32,16,256]{2,1,0:T(8,128)S(1)} %all_to_all.10.back_ref, s32[8,128]{1,0:T(8,128)S(1)} %get-tuple-element.14.dest_ref), custom_call_target="tpu_custom_call" | custom-call | tf_op jit(solution)/shard_map/home/pallas_call | solution.py:582
Async XLA Ops:
  4.6 14.6 %all-to-all-start = ((f32[8,16,256]{2,1,0:T(8,128)}), f32[8,16,256]{2,1,0:T(8,128)S(1)}, u32[]{:S(2)}, u32[]{:S(2)}) async-start(f32[8,16,256]{2,1,0:T(8,128)} %get-tuple-element.9), calls=%async_computation | async-start | bytes 262144 | tf_op jit(solution)/shard_map/all_to_all | solution.py:551
  11.9 0.8 %copy-start = (s32[8192]{0:T(1024)S(1)}, s32[8192]{0:T(1024)}, u32[]{:S(2)}) copy-start(s32[8192]{0:T(1024)} %param.7) | copy-start | bytes 98308
  12.6 0.7 %copy-start.1 = (s32[16]{0:T(128)S(1)}, s32[16]{0:T(128)}, u32[]{:S(2)}) copy-start(s32[16]{0:T(128)} %size_ref.1) | copy-start | bytes 196
  13.3 0.7 %copy-start.2 = (s32[16]{0:T(128)S(1)}, s32[16]{0:T(128)}, u32[]{:S(2)}) copy-start(s32[16]{0:T(128)} %owner_ref.1) | copy-start | bytes 196

commit v4 on v3

--- a/solution.py
+++ b/solution.py
@@ -57,18 +57,60 @@
     return as_bf16(iota((LANES, width), 0) < iota((LANES, width), 1))
 
 
+def lane_pick(value, index):
+    return jnp.take_along_axis(value, index, axis=1, mode="promise_in_bounds")
+
+
+def scatter(entries, steps, groups):
+    def add(g, total):
+        key, value = entries(g)
+        group = key >> 7
+        lane = key & (LANES - 1)
+        upper = (value >> 4).astype(jnp.float32)
+        lower = (value & 15).astype(jnp.float32)
+        lefts, rights = [], []
+        for s in range(8):
+            hit = iota((groups, LANES), 0) == group[s : s + 1]
+            lefts.append(
+                jnp.concatenate(
+                    [jnp.where(hit, upper[s : s + 1], 0.0), jnp.where(hit, lower[s : s + 1], 0.0)],
+                    axis=0,
+                ).astype(jnp.bfloat16)
+            )
+            rights.append(as_bf16(iota((LANES, LANES), 0) == lane[s : s + 1]))
+        return total + dot_bf16(
+            jnp.concatenate(lefts, axis=1), jnp.concatenate(rights, axis=1), NT
+        )
+
+    start = jnp.zeros((2 * groups, LANES), jnp.float32)
+    found = lax.fori_loop(0, steps, add, start, unroll=steps <= 8)
+    return (found[:groups] * 16.0 + found[groups:]).astype(jnp.int32)
+
+
+def take_columns(chunks, place):
+    place = jnp.broadcast_to(place, (8, LANES))
+    chunk = place >> 7
+    lane = place & (LANES - 1)
+    pieces = []
+    for v in range(chunks[0].shape[0] // 8):
+        taken = jnp.zeros((8, LANES), jnp.float32)
+        for c, value in enumerate(chunks):
+            taken = jnp.where(chunk == c, lane_pick(value[v * 8 : (v + 1) * 8], lane), taken)
+        pieces.append(taken)
+    return jnp.concatenate(pieces, axis=0)
+
+
 def pack_body(
     size_hbm,
     owner_hbm,
     x_hbm,
     perm_hbm,
     send_hbm,
-    dest_ref,
+    place_ref,
     size_ref,
     owner_ref,
     x_ref,
     perm_ref,
-    place_ref,
     send_ref,
     in_sems,
     out_sems,
@@ -95,8 +137,7 @@
     t_dev, ser_dev = x_ref.shape
     per_peer = SLOTS // n_ser
     shift = ser_dev.bit_length() - 1
-    groups = ser_dev // LANES
-    for load in loads[:3]:
+    for load in loads[:2]:
         load.wait()
 
     def owner_of(row_ids):
@@ -113,70 +154,41 @@
     earlier = as_bf16(
         (down_wide == owner_across) & (iota((rows, rows), 1) < iota((rows, rows), 0))
     )
+    loads[2].wait()
     mine = as_bf16((perm_ref[...] >> shift) == here)
     in_row = dot_bf16(mine, before_in_row(LANES))
     ahead = dot_bf16(earlier, mine).astype(jnp.bfloat16)
     in_rows = dot_bf16(ahead, jnp.ones((LANES, LANES), jnp.bfloat16))
     place_ref[...] = owner_down * per_peer + (in_row + in_rows).astype(jnp.int32)
 
-    def to_local(g, total):
+
+    def entries(g):
         at = pl.ds(pl.multiple_of(g * 8, 8), 8)
         series = perm_ref[at, :]
-        place = place_ref[at, :]
-        local = series & (ser_dev - 1)
-        group = jnp.where((series >> shift) == here, local >> 7, -1)
-        lane = local & (LANES - 1)
-        upper = (place >> 4).astype(jnp.float32)
-        lower = (place & 15).astype(jnp.float32)
-        lefts, rights = [], []
-        for s in range(8):
-            hit = iota((groups, LANES), 0) == group[s : s + 1]
-            lefts.append(
-                jnp.concatenate(
-                    [jnp.where(hit, upper[s : s + 1], 0.0), jnp.where(hit, lower[s : s + 1], 0.0)],
-                    axis=0,
-                ).astype(jnp.bfloat16)
-            )
-            rights.append(as_bf16(iota((LANES, LANES), 0) == lane[s : s + 1]))
-        return total + dot_bf16(
-            jnp.concatenate(lefts, axis=1), jnp.concatenate(rights, axis=1), NT
-        )
-
-    steps = rows // 8
-    found = lax.fori_loop(
-        0,
-        steps,
-        to_local,
-        jnp.zeros((2 * groups, LANES), jnp.float32),
-        unroll=steps <= 8,
-    )
-    dest = (found[:groups] * 16.0 + found[groups:]).astype(jnp.int32)
-    dest_ref[...] = dest
+        key = jnp.where((series >> shift) == here, place_ref[at, :], -1)
+        return key, (series & (ser_dev - 1)) + 1
+
+    column = scatter(entries, rows // 8, SLOTS // LANES) - 1
     loads[3].wait()
-    terms = split_three(x_ref[...])
-
-    def store(o, r):
-        return pltpu.make_async_copy(
-            send_ref.at[o], send_hbm.at[o], out_sems.at[o]
-        )
-
-    def pack(o, carry):
-        target = iota((per_peer, LANES), 0) + o * per_peer
-        pick = jnp.concatenate([as_bf16(target == dest[h : h + 1]) for h in range(groups)], axis=1)
-        send_ref[o] = join_three(dot_bf16(terms, pick, NT))
-        store(o, 0).start()
-        return carry
-
-    def finish(o, carry):
-        store(o, 0).wait()
-        return carry
-
-    lax.fori_loop(0, n_ser, pack, 0, unroll=n_ser <= 8)
-    lax.fori_loop(0, n_ser, finish, 0, unroll=n_ser <= 8)
-
-
-def lane_pick(value, index):
-    return jnp.take_along_axis(value, index, axis=1, mode="promise_in_bounds")
+    chunks = [x_ref[:, c * LANES : (c + 1) * LANES] for c in range(ser_dev // LANES)]
+    stores = [
+        pltpu.make_async_copy(send_ref.at[o], send_hbm.at[o], out_sems.at[o])
+        for o in range(n_ser)
+    ]
+    for k in range(SLOTS // LANES):
+        taken = take_columns(chunks, column[k : k + 1])
+        first = k * LANES // per_peer
+        if per_peer >= LANES:
+            start = k * LANES % per_peer
+            send_ref[first, :, start : start + LANES] = taken
+            if start + LANES == per_peer:
+                stores[first].start()
+        else:
+            for h in range(LANES // per_peer):
+                send_ref[first + h] = taken[:, h * per_peer : (h + 1) * per_peer]
+                stores[first + h].start()
+    for store in stores:
+        store.wait()
 
 
 def eliminate(parts, size, whole):
@@ -272,9 +284,11 @@
     size_ref,
     owner_ref,
     perm_ref,
+    place_ref,
     pick_ref,
     tile_of_ref,
     tile_ref,
+    dest_ref,
     index_ref,
     *,
     n_ser,
@@ -290,6 +304,13 @@
     shift = ser_dev.bit_length() - 1
     slot_rows = SLOTS // LANES
     wide = max(per_peer, LANES)
+
+    def entries(g):
+        at = pl.ds(pl.multiple_of(g * 8, 8), 8)
+        series = perm_ref[at, :]
+        return jnp.where((series >> shift) == here, series & (ser_dev - 1), -1), place_ref[at, :]
+
+    dest_ref[...] = scatter(entries, perm_ref.shape[0] // 8, ser_dev // LANES)
 
     for t in range(OWNER_TILES):
         tile_ref[0, t] = jnp.int32(-1)
@@ -499,18 +520,10 @@
         for q in range(1, n_org):
             piece = piece + back_ref[o * n_org + q]
         pieces.append(piece)
-    terms = split_three(jnp.concatenate(pieces, axis=1))
-    groups = dest_ref.shape[0]
-    step = 2
-    for h in range(0, groups, step):
-        pick = jnp.concatenate(
-            [
-                as_bf16(iota((SLOTS, LANES), 0) == dest_ref[h + i : h + i + 1, :])
-                for i in range(step)
-            ],
-            axis=1,
-        )
-        out_ref[:, h * LANES : (h + step) * LANES] = join_three(dot_bf16(terms, pick))
+    whole = jnp.concatenate(pieces, axis=1)
+    chunks = [whole[:, c * LANES : (c + 1) * LANES] for c in range(SLOTS // LANES)]
+    for h in range(dest_ref.shape[0]):
+        out_ref[:, h * LANES : (h + 1) * LANES] = take_columns(chunks, dest_ref[h : h + 1, :])
 
 
 def per_device(residual, sub_size, sub_owner, series_perm):
@@ -530,9 +543,9 @@
     params = pltpu.CompilerParams(vmem_limit_bytes=48 * 1024 * 1024)
     blocks_shape = jax.ShapeDtypeStruct((n_ser * n_org, t_dev, per_peer), jnp.float32)
 
-    send, dest = pl.pallas_call(
+    send, place = pl.pallas_call(
         functools.partial(pack_body, n_ser=n_ser, n_org=n_org),
-        out_shape=(jax.ShapeDtypeStruct((n_ser, t_dev, per_peer), jnp.float32), jax.ShapeDtypeStruct((ser_dev // LANES, LANES), jnp.int32)),
+        out_shape=(jax.ShapeDtypeStruct((n_ser, t_dev, per_peer), jnp.float32), jax.ShapeDtypeStruct(perm.shape, jnp.int32)),
         in_specs=[hbm, hbm, hbm, hbm],
         out_specs=(hbm, vmem),
         scratch_shapes=[
@@ -540,32 +553,32 @@
             pltpu.SMEM(sub_owner.shape, jnp.int32),
             pltpu.VMEM(residual.shape, jnp.float32),
             pltpu.VMEM(perm.shape, jnp.int32),
-            pltpu.VMEM(perm.shape, jnp.int32),
             pltpu.VMEM((n_ser, t_dev, per_peer), jnp.float32),
             pltpu.SemaphoreType.DMA((4,)),
-            pltpu.SemaphoreType.DMA((n_ser * n_org,)),
+            pltpu.SemaphoreType.DMA((n_ser,)),
         ],
         compiler_params=params,
         name="pack",
     )(to_hbm(sub_size), to_hbm(sub_owner), to_hbm(residual), to_hbm(perm))
     recv = lax.all_to_all(send, "ser", split_axis=0, concat_axis=0, tiled=True)
     recv = lax.all_gather(recv, "org", axis=0, tiled=True)
-    pick, tile_of, tile = pl.pallas_call(
+    pick, tile_of, tile, dest = pl.pallas_call(
         functools.partial(slots_body, n_ser=n_ser, n_org=n_org, ser_dev=ser_dev),
         out_shape=(
             jax.ShapeDtypeStruct((SLOTS, share), jnp.bfloat16),
             jax.ShapeDtypeStruct((1, SLOTS), jnp.int32),
             jax.ShapeDtypeStruct((3, OWNER_TILES), jnp.int32),
+            jax.ShapeDtypeStruct((ser_dev // LANES, LANES), jnp.int32),
         ),
-        in_specs=[smem, smem, vmem],
-        out_specs=(vmem, vmem, smem),
+        in_specs=[smem, smem, vmem, vmem],
+        out_specs=(vmem, vmem, smem, vmem),
         scratch_shapes=[pltpu.VMEM((SLOTS // LANES, LANES), jnp.int32)],
         compiler_params=params,
         cost_estimate=pl.CostEstimate(
             flops=4_000_000_000, bytes_accessed=4_000_000, transcendentals=0
         ),
         name="slots",
-    )(sub_size, sub_owner, perm)
+    )(sub_size, sub_owner, perm, place)
     back, log_part = pl.pallas_call(
         functools.partial(owner_body, n_ser=n_ser, n_org=n_org),
         out_shape=(blocks_shape, jax.ShapeDtypeStruct((1, share), jnp.float32)),

time: 55.9 us -> 55.1 us (0.986)
  Pallas kernels: 17.6 us -> 16.8 us
  waiting for transfers between devices: 3.18 us -> 2.56 us
  blocking collectives: 24.7 us -> 25.3 us
    pallas_call x1, Pallas kernels: 3.93 us -> 2.97 us  [per_device(): pl.pallas_call(functools.partial(pack_body, n_ser=n_ser, n_org=n_org), ou...]
    pallas_call x1, Pallas kernels: 2.08 us -> 2.7 us  [per_device(): pl.pallas_call(functools.partial(slots_body, n_ser=n_ser, n_org=n_org, se...]
    all_to_all x1, waiting for transfers between devices: 3.18 us -> 2.56 us  [per_device(): recv = lax.all_to_all(send, 'ser', split_axis=0, concat_axis=0, tiled=True)]
  transfers between devices with their start and end apart: 1 -> 1, of which waited for: 1 -> 1; matrix products, arithmetic and copies ran while one was open for 0% -> 0% of each run, Pallas kernels for 4% -> 5%
where the time goes in v4:
time: 55.1 us; the launch traced here: 54.7 us
  blocking collectives  25.3 us (46%)
  Pallas kernels  16.8 us (30%)
  starting transfers between devices  7.29 us (13%)
  waiting for transfers between devices  2.56 us (5%)
  local copies, waits for them, and re-layouts  2.06 us (4%)
  between operations  0.66 us (1%)
    all_to_all x1, blocking collectives, per_device(): lax.all_to_all(back, ('ser', 'org'), split_axis=0, concat_axis=0, tiled=T...  18.1 us
    pallas_call x1, Pallas kernels, per_device(): pl.pallas_call(functools.partial(owner_body, n_ser=n_ser, n_org=n_org), o...  10.2 us
    all_to_all x1, starting transfers between devices, per_device(): recv = lax.all_to_all(send, 'ser', split_axis=0, concat_axis=0, tiled=True)  7.29 us
    all_gather x1, blocking collectives, per_device(): recv = lax.all_gather(recv, 'org', axis=0, tiled=True)  7.16 us
    pallas_call x1, Pallas kernels, per_device(): pl.pallas_call(functools.partial(pack_body, n_ser=n_ser, n_org=n_org), ou...  2.97 us
    pallas_call x1, Pallas kernels, per_device(): pl.pallas_call(functools.partial(slots_body, n_ser=n_ser, n_org=n_org, se...  2.7 us
    all_to_all x1, waiting for transfers between devices, per_device(): recv = lax.all_to_all(send, 'ser', split_axis=0, concat_axis=0, tiled=True)  2.56 us
    unnamed x6, local copies, waits for them, and re-layouts  2.06 us
  transfers between devices with their start and end apart: 1, of which 1 were waited for; matrix products, arithmetic and copies ran while one was open for 0% of the time, Pallas kernels for 5%

profile of v4, /device:TPU:0, one launch (start us, length us, event | category | flops | bytes accessed | tf_op | source)
XLA Modules:
  0.0 54.7 jit_solution(17338231377219860719)
XLA Ops:
  0.6 3.0 %pack.1 = (f32[8,16,256]{2,1,0:T(8,128)}, s32[64,128]{1,0:T(8,128)S(1)}) custom-call(s32[16]{0:T(128)} %size_ref.1, s32[16]{0:T(128)} %owner_ref.1, f32[16,1024]{1,0:T(8,128)} %x_hbm.1, s32[64,128]{1,0:T(8,128)} %bitcast.1), custom_call_target="tpu_custom_call" | custom-call | tf_op jit(solution)/shard_map/pack/pallas_call | solution.py:546
  3.6 7.3 %all-to-all-start = ((f32[8,16,256]{2,1,0:T(8,128)}), f32[8,16,256]{2,1,0:T(8,128)S(1)}, u32[]{:S(2)}, u32[]{:S(2)}) async-start(f32[8,16,256]{2,1,0:T(8,128)} %get-tuple-element.10), calls=%async_computation | async-start | bytes 262144 | tf_op jit(solution)/shard_map/all_to_all | solution.py:563
  10.9 0.0 copy-start
  10.9 0.8 %copy-done = s32[8192]{0:T(1024)S(1)} copy-done((s32[8192]{0:T(1024)S(1)}, s32[8192]{0:T(1024)}, u32[]{:S(2)}) %copy-start) | copy-done | bytes 32792
  11.7 0.0 copy-start.1
  11.7 0.7 %copy-done.1 = s32[16]{0:T(128)S(1)} copy-done((s32[16]{0:T(128)S(1)}, s32[16]{0:T(128)}, u32[]{:S(2)}) %copy-start.1) | copy-done | bytes 88
  12.3 0.0 copy-start.2
  12.3 0.7 %copy-done.2 = s32[16]{0:T(128)S(1)} copy-done((s32[16]{0:T(128)S(1)}, s32[16]{0:T(128)}, u32[]{:S(2)}) %copy-start.2) | copy-done | bytes 88
  13.0 2.7 %slots.1 = (bf16[2048,512]{1,0:T(8,128)(2,1)S(1)}, s32[1,2048]{1,0:T(1,128)S(1)}, s32[3,8]{1,0:T(4,128)S(1)}, s32[8,128]{1,0:T(8,128)S(1)}) custom-call(s32[16]{0:T(128)S(1)} %copy-done.1, s32[16]{0:T(128)S(1)} %copy-done.2, s32[64,128]{1,0:T(8,128)S(1)} %bitcast.2, s32[64,128]{1,0:T(8,128)S(1)} %get-tuple-element.11.place_ref), custom_call_target="tpu_custom_call" | custom-call | flops 4000000000 | bytes 4000000 | tf_op jit(solution)/shard_map/slots/pallas_call | solution.py:565
  15.7 2.6 %all-to-all-done = f32[8,16,256]{2,1,0:T(8,128)S(1)} async-done(((f32[8,16,256]{2,1,0:T(8,128)}), f32[8,16,256]{2,1,0:T(8,128)S(1)}, u32[]{:S(2)}, u32[]{:S(2)}) %all-to-all-start) | async-done | bytes 131104 | tf_op jit(solution)/shard_map/all_to_all | solution.py:563
  18.2 7.2 %all_gather.3.recv_ref = f32[32,16,256]{2,1,0:T(8,128)S(1)} all-gather(f32[8,16,256]{2,1,0:T(8,128)S(1)} %all-to-all-done), channel_id=1, replica_groups=mesh['ser'=8,'org'=4] {'org'}, dimensions={0}, use_global_device_ids=true | all-gather | bytes 655360 | tf_op jit(solution)/shard_map/all_gather | solution.py:564
  25.4 10.2 %owner.1 = (f32[32,16,256]{2,1,0:T(8,128)S(1)}, f32[1,512]{1,0:T(1,128)}) custom-call(f32[32,16,256]{2,1,0:T(8,128)S(1)} %all_gather.3.recv_ref, bf16[2048,512]{1,0:T(8,128)(2,1)S(1)} %get-tuple-element.12.pick_ref, s32[1,2048]{1,0:T(1,128)S(1)} %get-tuple-element.13.tile_of_ref, s32[3,8]{1,0:T(4,128)S(1)} %get-tuple-element.14.tile_ref), custom_call_target="tpu_custom_call" | custom-call | tf_op jit(solution)/shard_map/owner/pallas_call | solution.py:582
  35.6 18.1 %all_to_all.10.back_ref = f32[32,16,256]{2,1,0:T(8,128)S(1)} all-to-all(f32[32,16,256]{2,1,0:T(8,128)S(1)} %get-tuple-element.15), channel_id=1, replica_groups=mesh['ser'=8,'org'=4] {'ser','org'}, dimensions={0} | all-to-all | bytes 1048576 | tf_op jit(solution)/shard_map/all_to_all | solution.py:594
  53.7 1.0 %home.1 = f32[16,1024]{1,0:T(8,128)} custom-call(f32[32,16,256]{2,1,0:T(8,128)S(1)} %all_to_all.10.back_ref, s32[8,128]{1,0:T(8,128)S(1)} %get-tuple-element.16.dest_ref), custom_call_target="tpu_custom_call" | custom-call | tf_op jit(solution)/shard_map/home/pallas_call | solution.py:595
Async XLA Ops:
  3.6 14.6 %all-to-all-start = ((f32[8,16,256]{2,1,0:T(8,128)}), f32[8,16,256]{2,1,0:T(8,128)S(1)}, u32[]{:S(2)}, u32[]{:S(2)}) async-start(f32[8,16,256]{2,1,0:T(8,128)} %get-tuple-element.10), calls=%async_computation | async-start | bytes 262144 | tf_op jit(solution)/shard_map/all_to_all | solution.py:563
  10.9 0.8 %copy-start = (s32[8192]{0:T(1024)S(1)}, s32[8192]{0:T(1024)}, u32[]{:S(2)}) copy-start(s32[8192]{0:T(1024)} %param.7) | copy-start | bytes 98308
  11.7 0.7 %copy-start.1 = (s32[16]{0:T(128)S(1)}, s32[16]{0:T(128)}, u32[]{:S(2)}) copy-start(s32[16]{0:T(128)} %size_ref.1) | copy-start | bytes 196
  12.3 0.7 %copy-start.2 = (s32[16]{0:T(128)S(1)}, s32[16]{0:T(128)}, u32[]{:S(2)}) copy-start(s32[16]{0:T(128)} %owner_ref.1) | copy-start | bytes 196

commit v5 on v4

--- a/solution.py
+++ b/solution.py
@@ -237,12 +237,12 @@
                     rows.append(row)
                 for a in reversed(range(count)):
                     row = rows[a] * inv[a]
-                    for b in range(a + 1, count):
+                    for b in reversed(range(a + 1, count)):
                         row = row - low[b][a] * solved[b]
                     solved[a] = row
                 for v in range(tall):
                     new = jnp.where(on, 0.0, panel[v])
-                    for a in range(count):
+                    for a in reversed(range(count)):
                         new = new - picked[v][a] * solved[a]
                     if v == g:
                         for a in range(count):
@@ -369,31 +369,20 @@
         pick_ref[:, i * LANES : (i + 1) * LANES] = as_bf16(iota((SLOTS, LANES), 0) == row)
 
 
-def owner_body(
-    recv_ref,
-    pick_ref,
-    tile_of_ref,
-    tile_ref,
-    back_ref,
-    log_ref,
-    all_ref,
-    inverse_ref,
-    *,
-    n_ser,
-    n_org,
-):
+def owner_body(*refs, n_ser, n_org, flips):
+    recv_refs = refs[:n_org]
+    pick_ref, tile_of_ref, tile_ref, back_ref, log_ref, all_ref, inverse_ref = refs[n_org:]
     part = lax.axis_index("org")
-    t_dev = recv_ref.shape[1]
+    t_dev = recv_refs[0].shape[1]
     anchors = t_dev * n_org
     per_peer = SLOTS // n_ser
     share = SLOTS // n_org
     tiles = share // TILE
 
-    for d in range(n_ser):
-        for r in range(n_org):
-            all_ref[r * t_dev : (r + 1) * t_dev, d * per_peer : (d + 1) * per_peer] = recv_ref[
-                r * n_ser + d
-            ]
+    for flip, part_ref in zip(flips, recv_refs):
+        row = pl.multiple_of((part ^ flip) * t_dev, t_dev)
+        for d in range(n_ser):
+            all_ref[pl.ds(row, t_dev), d * per_peer : (d + 1) * per_peer] = part_ref[d]
 
     tile_of = tile_of_ref[...]
 
@@ -561,7 +550,6 @@
         name="pack",
     )(to_hbm(sub_size), to_hbm(sub_owner), to_hbm(residual), to_hbm(perm))
     recv = lax.all_to_all(send, "ser", split_axis=0, concat_axis=0, tiled=True)
-    recv = lax.all_gather(recv, "org", axis=0, tiled=True)
     pick, tile_of, tile, dest = pl.pallas_call(
         functools.partial(slots_body, n_ser=n_ser, n_org=n_org, ser_dev=ser_dev),
         out_shape=(
@@ -579,10 +567,19 @@
         ),
         name="slots",
     )(sub_size, sub_owner, perm, place)
+    recv, pick, tile_of, tile, dest = lax.optimization_barrier(
+        (recv, pick, tile_of, tile, dest)
+    )
+    received, flips, bit = [recv], [0], n_org // 2
+    while bit:
+        swap = [(i, i ^ bit) for i in range(n_org)]
+        received = received + [lax.ppermute(part, "org", swap) for part in received]
+        flips = flips + [flip ^ bit for flip in flips]
+        bit //= 2
     back, log_part = pl.pallas_call(
-        functools.partial(owner_body, n_ser=n_ser, n_org=n_org),
+        functools.partial(owner_body, n_ser=n_ser, n_org=n_org, flips=flips),
         out_shape=(blocks_shape, jax.ShapeDtypeStruct((1, share), jnp.float32)),
-        in_specs=[vmem, vmem, vmem, smem],
+        in_specs=[vmem] * n_org + [vmem, vmem, smem],
         out_specs=(vmem, vmem),
         scratch_shapes=[
             pltpu.VMEM((anchors, SLOTS), jnp.float32),
@@ -590,7 +587,7 @@
         ],
         compiler_params=params,
         name="owner",
-    )(recv, pick, tile_of, tile)
+    )(*received, pick, tile_of, tile)
     returned = lax.all_to_all(back, ("ser", "org"), split_axis=0, concat_axis=0, tiled=True)
     whitened = pl.pallas_call(
         functools.partial(home_body, n_ser=n_ser, n_org=n_org),

time: 55.1 us -> 54.7 us (level)
  blocking collectives: 25.3 us -> 18.8 us
  waiting for transfers between devices: 2.56 us -> 7.4 us
  starting transfers between devices: 7.29 us -> 8.79 us
    all_gather x1 -> x0, blocking collectives: 7.16 us -> none  [per_device(): recv = lax.all_gather(recv, 'org', axis=0, tiled=True)]
    ppermute x0 -> x3, waiting for transfers between devices: none -> 4.82 us  [per_device(): received = received + [lax.ppermute(part, 'org', swap) for part in received]]
    ppermute x0 -> x3, starting transfers between devices: none -> 1.5 us  [per_device(): received = received + [lax.ppermute(part, 'org', swap) for part in received]]
    all_to_all x1, blocking collectives: 18.1 us -> 18.8 us  [per_device(): lax.all_to_all(back, ('ser', 'org'), split_axis=0, concat_axis=0, tiled=T...]
  transfers between devices with their start and end apart: 1 -> 4, of which waited for: 1 -> 3; matrix products, arithmetic and copies ran while one was open for 0% -> 0% of each run, Pallas kernels for 5% -> 5%
where the time goes in v5:
time: 54.7 us; the launch traced here: 54.4 us
  blocking collectives  18.8 us (34%)
  Pallas kernels  16.6 us (30%)
  starting transfers between devices  8.79 us (16%)
  waiting for transfers between devices  7.4 us (14%)
  local copies, waits for them, and re-layouts  2.06 us (4%)
  between operations  0.66 us (1%)
    all_to_all x1, blocking collectives, per_device(): lax.all_to_all(back, ('ser', 'org'), split_axis=0, concat_axis=0, tiled=T...  18.8 us
    pallas_call x1, Pallas kernels, per_device(): pl.pallas_call(functools.partial(owner_body, n_ser=n_ser, n_org=n_org, fl...  9.99 us
    all_to_all x1, starting transfers between devices, per_device(): recv = lax.all_to_all(send, 'ser', split_axis=0, concat_axis=0, tiled=True)  7.29 us
    ppermute x3, waiting for transfers between devices, per_device(): received = received + [lax.ppermute(part, 'org', swap) for part in received]  4.82 us
    pallas_call x1, Pallas kernels, per_device(): pl.pallas_call(functools.partial(pack_body, n_ser=n_ser, n_org=n_org), ou...  2.98 us
    pallas_call x1, Pallas kernels, per_device(): pl.pallas_call(functools.partial(slots_body, n_ser=n_ser, n_org=n_org, se...  2.68 us
    all_to_all x1, waiting for transfers between devices, per_device(): recv = lax.all_to_all(send, 'ser', split_axis=0, concat_axis=0, tiled=True)  2.58 us
    unnamed x6, local copies, waits for them, and re-layouts  2.06 us
  transfers between devices with their start and end apart: 4, of which 3 were waited for; matrix products, arithmetic and copies ran while one was open for 0% of the time, Pallas kernels for 5%

profile of v5, /device:TPU:0, one launch (start us, length us, event | category | flops | bytes accessed | tf_op | source)
XLA Modules:
  0.0 54.4 jit_solution(17244817030447072778)
XLA Ops:
  0.6 3.0 %pack.1 = (f32[8,16,256]{2,1,0:T(8,128)}, s32[64,128]{1,0:T(8,128)S(1)}) custom-call(s32[16]{0:T(128)} %size_ref.1, s32[16]{0:T(128)} %owner_ref.1, f32[16,1024]{1,0:T(8,128)} %x_hbm.1, s32[64,128]{1,0:T(8,128)} %bitcast.1), custom_call_target="tpu_custom_call" | custom-call | tf_op jit(solution)/shard_map/pack/pallas_call | solution.py:535
  3.6 7.3 %all-to-all-start = ((f32[8,16,256]{2,1,0:T(8,128)}), f32[8,16,256]{2,1,0:T(8,128)S(1)}, u32[]{:S(2)}, u32[]{:S(2)}) async-start(f32[8,16,256]{2,1,0:T(8,128)} %get-tuple-element.15), calls=%async_computation | async-start | bytes 262144 | tf_op jit(solution)/shard_map/all_to_all | solution.py:552
  10.9 0.0 copy-start
  10.9 0.8 %copy-done = s32[8192]{0:T(1024)S(1)} copy-done((s32[8192]{0:T(1024)S(1)}, s32[8192]{0:T(1024)}, u32[]{:S(2)}) %copy-start) | copy-done | bytes 32792
  11.7 0.0 copy-start.1
  11.7 0.7 %copy-done.1 = s32[16]{0:T(128)S(1)} copy-done((s32[16]{0:T(128)S(1)}, s32[16]{0:T(128)}, u32[]{:S(2)}) %copy-start.1) | copy-done | bytes 88
  12.3 0.0 copy-start.2
  12.3 0.7 %copy-done.2 = s32[16]{0:T(128)S(1)} copy-done((s32[16]{0:T(128)S(1)}, s32[16]{0:T(128)}, u32[]{:S(2)}) %copy-start.2) | copy-done | bytes 88
  13.0 2.7 %slots.1 = (bf16[2048,512]{1,0:T(8,128)(2,1)S(1)}, s32[1,2048]{1,0:T(1,128)S(1)}, s32[3,8]{1,0:T(4,128)S(1)}, s32[8,128]{1,0:T(8,128)S(1)}) custom-call(s32[16]{0:T(128)S(1)} %copy-done.1, s32[16]{0:T(128)S(1)} %copy-done.2, s32[64,128]{1,0:T(8,128)S(1)} %bitcast.2, s32[64,128]{1,0:T(8,128)S(1)} %get-tuple-element.16.place_ref), custom_call_target="tpu_custom_call" | custom-call | flops 4000000000 | bytes 4000000 | tf_op jit(solution)/shard_map/slots/pallas_call | solution.py:553
  15.7 2.6 %all-to-all-done.refs_0_ = f32[8,16,256]{2,1,0:T(8,128)S(1)} async-done(((f32[8,16,256]{2,1,0:T(8,128)}), f32[8,16,256]{2,1,0:T(8,128)S(1)}, u32[]{:S(2)}, u32[]{:S(2)}) %all-to-all-start) | async-done | bytes 131104 | tf_op jit(solution)/shard_map/all_to_all | solution.py:552
  18.2 1.5 %collective-permute-start = (f32[8,16,256]{2,1,0:T(8,128)S(1)}, f32[8,16,256]{2,1,0:T(8,128)S(1)}, u32[]{:S(2)}, u32[]{:S(2)}) collective-permute-start(f32[8,16,256]{2,1,0:T(8,128)S(1)} %all-to-all-done.refs_0_), channel_id=1, source_target_pairs={{0,2},{1,3},{2,0},{3,1},{4,6},{5,7},{6,4},{7,5},{8,10},{9,11},{10,... | collective-permute-start | bytes 393224 | tf_op jit(solution)/shard_map/ppermute | solution.py:576
  19.7 0.0 collective-permute-start.1
  19.7 3.5 %collective-permute-done.refs_1_ = f32[8,16,256]{2,1,0:T(8,128)S(1)} collective-permute-done((f32[8,16,256]{2,1,0:T(8,128)S(1)}, f32[8,16,256]{2,1,0:T(8,128)S(1)}, u32[]{:S(2)}, u32[]{:S(2)}) %collective-permute-start) | collective-permute-done | bytes 131104 | tf_op jit(solution)/shard_map/ppermute | solution.py:576
  23.2 0.0 collective-permute-start.2
  23.2 0.0 collective-permute-done.1.refs_2_
  23.2 1.3 %collective-permute-done.2.refs_3_ = f32[8,16,256]{2,1,0:T(8,128)S(1)} collective-permute-done((f32[8,16,256]{2,1,0:T(8,128)S(1)}, f32[8,16,256]{2,1,0:T(8,128)S(1)}, u32[]{:S(2)}, u32[]{:S(2)}) %collective-permute-start.2) | collective-permute-done | bytes 131104 | tf_op jit(solution)/shard_map/ppermute | solution.py:576
  24.6 10.0 %owner.1 = (f32[32,16,256]{2,1,0:T(8,128)S(1)}, f32[1,512]{1,0:T(1,128)}) custom-call(f32[8,16,256]{2,1,0:T(8,128)S(1)} %all-to-all-done.refs_0_, f32[8,16,256]{2,1,0:T(8,128)S(1)} %collective-permute-done.refs_1_, f32[8,16,256]{2,1,0:T(8,128)S(1)} %collective-permute-done.1.refs_2_, f32[8,16,256]{2,1,0:T(8,128)S(1)} %collective-permute-done.2.refs_3_, ...), custom_call_target="tpu_custom_call" | custom-call | tf_op jit(solution)/shard_map/owner/pallas_call | solution.py:579
  34.6 18.8 %all_to_all.10.back_ref = f32[32,16,256]{2,1,0:T(8,128)S(1)} all-to-all(f32[32,16,256]{2,1,0:T(8,128)S(1)} %get-tuple-element.25), channel_id=1, replica_groups=mesh['ser'=8,'org'=4] {'ser','org'}, dimensions={0} | all-to-all | bytes 1048576 | tf_op jit(solution)/shard_map/all_to_all | solution.py:591
  53.4 1.0 %home.1 = f32[16,1024]{1,0:T(8,128)} custom-call(f32[32,16,256]{2,1,0:T(8,128)S(1)} %all_to_all.10.back_ref, s32[8,128]{1,0:T(8,128)S(1)} %get-tuple-element.26.dest_ref), custom_call_target="tpu_custom_call" | custom-call | tf_op jit(solution)/shard_map/home/pallas_call | solution.py:592
Async XLA Ops:
  3.6 14.6 %all-to-all-start = ((f32[8,16,256]{2,1,0:T(8,128)}), f32[8,16,256]{2,1,0:T(8,128)S(1)}, u32[]{:S(2)}, u32[]{:S(2)}) async-start(f32[8,16,256]{2,1,0:T(8,128)} %get-tuple-element.15), calls=%async_computation | async-start | bytes 262144 | tf_op jit(solution)/shard_map/all_to_all | solution.py:552
  10.9 0.8 %copy-start = (s32[8192]{0:T(1024)S(1)}, s32[8192]{0:T(1024)}, u32[]{:S(2)}) copy-start(s32[8192]{0:T(1024)} %param.7) | copy-start | bytes 98308
  11.7 0.7 %copy-start.1 = (s32[16]{0:T(128)S(1)}, s32[16]{0:T(128)}, u32[]{:S(2)}) copy-start(s32[16]{0:T(128)} %size_ref.1) | copy-start | bytes 196
  12.3 0.7 %copy-start.2 = (s32[16]{0:T(128)S(1)}, s32[16]{0:T(128)}, u32[]{:S(2)}) copy-start(s32[16]{0:T(128)} %owner_ref.1) | copy-start | bytes 196
  18.2 5.0 %collective-permute-start = (f32[8,16,256]{2,1,0:T(8,128)S(1)}, f32[8,16,256]{2,1,0:T(8,128)S(1)}, u32[]{:S(2)}, u32[]{:S(2)}) collective-permute-start(f32[8,16,256]{2,1,0:T(8,128)S(1)} %all-to-all-done.refs_0_), channel_id=1, source_target_pairs={{0,2},{1,3},{2,0},{3,1},{4,6},{5,7},{6,4},{7,5},{8,10},{9,11},{10,... | collective-permute-start | bytes 393224 | tf_op jit(solution)/shard_map/ppermute | solution.py:576
  19.7 3.5 %collective-permute-start.1 = (f32[8,16,256]{2,1,0:T(8,128)S(1)}, f32[8,16,256]{2,1,0:T(8,128)S(1)}, u32[]{:S(2)}, u32[]{:S(2)}) collective-permute-start(f32[8,16,256]{2,1,0:T(8,128)S(1)} %all-to-all-done.refs_0_), channel_id=1, source_target_pairs={{0,1},{1,0},{2,3},{3,2},{4,5},{5,4},{6,7},{7,6},{8,9},{9,8},{10,11... | collective-permute-start | bytes 393224 | tf_op jit(solution)/shard_map/ppermute | solution.py:576
  23.2 1.3 %collective-permute-start.2 = (f32[8,16,256]{2,1,0:T(8,128)S(1)}, f32[8,16,256]{2,1,0:T(8,128)S(1)}, u32[]{:S(2)}, u32[]{:S(2)}) collective-permute-start(f32[8,16,256]{2,1,0:T(8,128)S(1)} %collective-permute-done.refs_1_), channel_id=1, source_target_pairs={{0,1},{1,0},{2,3},{3,2},{4,5},{5,4},{6,7},{7,6},{8,9},{9,8},{10,11... | collective-permute-start | bytes 393224 | tf_op jit(solution)/shard_map/ppermute | solution.py:576

commit v6 on v5

--- a/solution.py
+++ b/solution.py
@@ -241,6 +241,12 @@
                         row = row - low[b][a] * solved[b]
                     solved[a] = row
                 for v in range(tall):
+                    if v == g and count == 8:
+                        new = solved[0]
+                        for a in range(1, count):
+                            new = jnp.where(sub == a, solved[a], new)
+                        panel[v] = new
+                        continue
                     new = jnp.where(on, 0.0, panel[v])
                     for a in reversed(range(count)):
                         new = new - picked[v][a] * solved[a]
@@ -249,9 +255,9 @@
                             new = jnp.where(sub == s + a, solved[a], new)
                     panel[v] = new
                 if not whole:
-                    for v in range(g, tall):
-                        ahead = (sub >= s + count) | (v > g)
-                        kept[p][v] = jnp.where(ahead, panel[v], kept[p][v])
+                    if count < 8:
+                        kept[p][g] = jnp.where(sub >= s + count, panel[g], kept[p][g])
+                    kept[p][g + 1 :] = panel[g + 1 :]
                     for a in range(count):
                         here = sub == s + a
                         pivot = corner[a][a]

time: 54.7 us -> 54.6 us (level)
  no operation moved by 1% of the time
where the time goes in v6:
time: 54.6 us; the launch traced here: 54.3 us
  blocking collectives  18.8 us (34%)
  Pallas kernels  16.5 us (30%)
  starting transfers between devices  8.79 us (16%)
  waiting for transfers between devices  7.37 us (13%)
  local copies, waits for them, and re-layouts  2.06 us (4%)
  between operations  0.66 us (1%)
    all_to_all x1, blocking collectives, per_device(): lax.all_to_all(back, ('ser', 'org'), split_axis=0, concat_axis=0, tiled=T...  18.8 us
    pallas_call x1, Pallas kernels, per_device(): pl.pallas_call(functools.partial(owner_body, n_ser=n_ser, n_org=n_org, fl...  9.87 us
    all_to_all x1, starting transfers between devices, per_device(): recv = lax.all_to_all(send, 'ser', split_axis=0, concat_axis=0, tiled=True)  7.29 us
    ppermute x3, waiting for transfers between devices, per_device(): received = received + [lax.ppermute(part, 'org', swap) for part in received]  4.82 us
    pallas_call x1, Pallas kernels, per_device(): pl.pallas_call(functools.partial(pack_body, n_ser=n_ser, n_org=n_org), ou...  2.98 us
    pallas_call x1, Pallas kernels, per_device(): pl.pallas_call(functools.partial(slots_body, n_ser=n_ser, n_org=n_org, se...  2.71 us
    all_to_all x1, waiting for transfers between devices, per_device(): recv = lax.all_to_all(send, 'ser', split_axis=0, concat_axis=0, tiled=True)  2.56 us
    unnamed x6, local copies, waits for them, and re-layouts  2.06 us
  transfers between devices with their start and end apart: 4, of which 3 were waited for; matrix products, arithmetic and copies ran while one was open for 0% of the time, Pallas kernels for 5%

profile of v6, /device:TPU:0, one launch (start us, length us, event | category | flops | bytes accessed | tf_op | source)
XLA Modules:
  0.0 54.3 jit_solution(7210886176641825713)
XLA Ops:
  0.6 3.0 %pack.1 = (f32[8,16,256]{2,1,0:T(8,128)}, s32[64,128]{1,0:T(8,128)S(1)}) custom-call(s32[16]{0:T(128)} %size_ref.1, s32[16]{0:T(128)} %owner_ref.1, f32[16,1024]{1,0:T(8,128)} %x_hbm.1, s32[64,128]{1,0:T(8,128)} %bitcast.1), custom_call_target="tpu_custom_call" | custom-call | tf_op jit(solution)/shard_map/pack/pallas_call | solution.py:541
  3.6 7.3 %all-to-all-start = ((f32[8,16,256]{2,1,0:T(8,128)}), f32[8,16,256]{2,1,0:T(8,128)S(1)}, u32[]{:S(2)}, u32[]{:S(2)}) async-start(f32[8,16,256]{2,1,0:T(8,128)} %get-tuple-element.15), calls=%async_computation | async-start | bytes 262144 | tf_op jit(solution)/shard_map/all_to_all | solution.py:558
  10.9 0.0 copy-start
  10.9 0.8 %copy-done = s32[8192]{0:T(1024)S(1)} copy-done((s32[8192]{0:T(1024)S(1)}, s32[8192]{0:T(1024)}, u32[]{:S(2)}) %copy-start) | copy-done | bytes 32792
  11.7 0.0 copy-start.1
  11.7 0.7 %copy-done.1 = s32[16]{0:T(128)S(1)} copy-done((s32[16]{0:T(128)S(1)}, s32[16]{0:T(128)}, u32[]{:S(2)}) %copy-start.1) | copy-done | bytes 88
  12.3 0.0 copy-start.2
  12.3 0.7 %copy-done.2 = s32[16]{0:T(128)S(1)} copy-done((s32[16]{0:T(128)S(1)}, s32[16]{0:T(128)}, u32[]{:S(2)}) %copy-start.2) | copy-done | bytes 88
  13.0 2.7 %slots.1 = (bf16[2048,512]{1,0:T(8,128)(2,1)S(1)}, s32[1,2048]{1,0:T(1,128)S(1)}, s32[3,8]{1,0:T(4,128)S(1)}, s32[8,128]{1,0:T(8,128)S(1)}) custom-call(s32[16]{0:T(128)S(1)} %copy-done.1, s32[16]{0:T(128)S(1)} %copy-done.2, s32[64,128]{1,0:T(8,128)S(1)} %bitcast.2, s32[64,128]{1,0:T(8,128)S(1)} %get-tuple-element.16.place_ref), custom_call_target="tpu_custom_call" | custom-call | flops 4000000000 | bytes 4000000 | tf_op jit(solution)/shard_map/slots/pallas_call | solution.py:559
  15.7 2.6 %all-to-all-done.refs_0_ = f32[8,16,256]{2,1,0:T(8,128)S(1)} async-done(((f32[8,16,256]{2,1,0:T(8,128)}), f32[8,16,256]{2,1,0:T(8,128)S(1)}, u32[]{:S(2)}, u32[]{:S(2)}) %all-to-all-start) | async-done | bytes 131104 | tf_op jit(solution)/shard_map/all_to_all | solution.py:558
  18.2 1.5 %collective-permute-start = (f32[8,16,256]{2,1,0:T(8,128)S(1)}, f32[8,16,256]{2,1,0:T(8,128)S(1)}, u32[]{:S(2)}, u32[]{:S(2)}) collective-permute-start(f32[8,16,256]{2,1,0:T(8,128)S(1)} %all-to-all-done.refs_0_), channel_id=1, source_target_pairs={{0,2},{1,3},{2,0},{3,1},{4,6},{5,7},{6,4},{7,5},{8,10},{9,11},{10,... | collective-permute-start | bytes 393224 | tf_op jit(solution)/shard_map/ppermute | solution.py:582
  19.7 0.0 collective-permute-start.1
  19.7 3.5 %collective-permute-done.refs_1_ = f32[8,16,256]{2,1,0:T(8,128)S(1)} collective-permute-done((f32[8,16,256]{2,1,0:T(8,128)S(1)}, f32[8,16,256]{2,1,0:T(8,128)S(1)}, u32[]{:S(2)}, u32[]{:S(2)}) %collective-permute-start) | collective-permute-done | bytes 131104 | tf_op jit(solution)/shard_map/ppermute | solution.py:582
  23.2 0.0 collective-permute-start.2
  23.2 0.0 collective-permute-done.1.refs_2_
  23.2 1.3 %collective-permute-done.2.refs_3_ = f32[8,16,256]{2,1,0:T(8,128)S(1)} collective-permute-done((f32[8,16,256]{2,1,0:T(8,128)S(1)}, f32[8,16,256]{2,1,0:T(8,128)S(1)}, u32[]{:S(2)}, u32[]{:S(2)}) %collective-permute-start.2) | collective-permute-done | bytes 131104 | tf_op jit(solution)/shard_map/ppermute | solution.py:582
  24.6 9.9 %owner.1 = (f32[32,16,256]{2,1,0:T(8,128)S(1)}, f32[1,512]{1,0:T(1,128)}) custom-call(f32[8,16,256]{2,1,0:T(8,128)S(1)} %all-to-all-done.refs_0_, f32[8,16,256]{2,1,0:T(8,128)S(1)} %collective-permute-done.refs_1_, f32[8,16,256]{2,1,0:T(8,128)S(1)} %collective-permute-done.1.refs_2_, f32[8,16,256]{2,1,0:T(8,128)S(1)} %collective-permute-done.2.refs_3_, ...), custom_call_target="tpu_custom_call" | custom-call | tf_op jit(solution)/shard_map/owner/pallas_call | solution.py:585
  34.4 18.8 %all_to_all.10.back_ref = f32[32,16,256]{2,1,0:T(8,128)S(1)} all-to-all(f32[32,16,256]{2,1,0:T(8,128)S(1)} %get-tuple-element.25), channel_id=1, replica_groups=mesh['ser'=8,'org'=4] {'ser','org'}, dimensions={0} | all-to-all | bytes 1048576 | tf_op jit(solution)/shard_map/all_to_all | solution.py:597
  53.3 1.0 %home.1 = f32[16,1024]{1,0:T(8,128)} custom-call(f32[32,16,256]{2,1,0:T(8,128)S(1)} %all_to_all.10.back_ref, s32[8,128]{1,0:T(8,128)S(1)} %get-tuple-element.26.dest_ref), custom_call_target="tpu_custom_call" | custom-call | tf_op jit(solution)/shard_map/home/pallas_call | solution.py:598
Async XLA Ops:
  3.6 14.6 %all-to-all-start = ((f32[8,16,256]{2,1,0:T(8,128)}), f32[8,16,256]{2,1,0:T(8,128)S(1)}, u32[]{:S(2)}, u32[]{:S(2)}) async-start(f32[8,16,256]{2,1,0:T(8,128)} %get-tuple-element.15), calls=%async_computation | async-start | bytes 262144 | tf_op jit(solution)/shard_map/all_to_all | solution.py:558
  10.9 0.8 %copy-start = (s32[8192]{0:T(1024)S(1)}, s32[8192]{0:T(1024)}, u32[]{:S(2)}) copy-start(s32[8192]{0:T(1024)} %param.7) | copy-start | bytes 98308
  11.7 0.7 %copy-start.1 = (s32[16]{0:T(128)S(1)}, s32[16]{0:T(128)}, u32[]{:S(2)}) copy-start(s32[16]{0:T(128)} %size_ref.1) | copy-start | bytes 196
  12.3 0.7 %copy-start.2 = (s32[16]{0:T(128)S(1)}, s32[16]{0:T(128)}, u32[]{:S(2)}) copy-start(s32[16]{0:T(128)} %owner_ref.1) | copy-start | bytes 196
  18.2 5.0 %collective-permute-start = (f32[8,16,256]{2,1,0:T(8,128)S(1)}, f32[8,16,256]{2,1,0:T(8,128)S(1)}, u32[]{:S(2)}, u32[]{:S(2)}) collective-permute-start(f32[8,16,256]{2,1,0:T(8,128)S(1)} %all-to-all-done.refs_0_), channel_id=1, source_target_pairs={{0,2},{1,3},{2,0},{3,1},{4,6},{5,7},{6,4},{7,5},{8,10},{9,11},{10,... | collective-permute-start | bytes 393224 | tf_op jit(solution)/shard_map/ppermute | solution.py:582
  19.7 3.5 %collective-permute-start.1 = (f32[8,16,256]{2,1,0:T(8,128)S(1)}, f32[8,16,256]{2,1,0:T(8,128)S(1)}, u32[]{:S(2)}, u32[]{:S(2)}) collective-permute-start(f32[8,16,256]{2,1,0:T(8,128)S(1)} %all-to-all-done.refs_0_), channel_id=1, source_target_pairs={{0,1},{1,0},{2,3},{3,2},{4,5},{5,4},{6,7},{7,6},{8,9},{9,8},{10,11... | collective-permute-start | bytes 393224 | tf_op jit(solution)/shard_map/ppermute | solution.py:582
  23.2 1.3 %collective-permute-start.2 = (f32[8,16,256]{2,1,0:T(8,128)S(1)}, f32[8,16,256]{2,1,0:T(8,128)S(1)}, u32[]{:S(2)}, u32[]{:S(2)}) collective-permute-start(f32[8,16,256]{2,1,0:T(8,128)S(1)} %collective-permute-done.refs_1_), channel_id=1, source_target_pairs={{0,1},{1,0},{2,3},{3,2},{4,5},{5,4},{6,7},{7,6},{8,9},{9,8},{10,11... | collective-permute-start | bytes 393224 | tf_op jit(solution)/shard_map/ppermute | solution.py:582
